TPU v7x, 256 devices: a whole 4x4x8 slice. The times are simulated.
256 devices in a mesh: lon: 32 (over z, x_lo, core), lat: 8 (over x_hi, y).
Axes of the slice: x: 4 (x_hi: 2, x_lo: 2; x = x_hi * 2 + x_lo), y: 4, z: 8, core: 2. Of those that a mesh axis runs over, the one named last changes fastest.
Arguments:
- increment: float32 [2, 512, 4096], P(None, 'lat', 'lon'), may hold values from -6 to 6
- members: bfloat16 [32, 2, 512, 4096], P(None, None, 'lat', 'lon'), may hold values from -6 to 6
- climate_spread: float32 [2, 512, 4096], P(None, 'lat', 'lon'), may hold values from 0.5 to 2
- diffusivity: float32 [512, 4096], P('lat', 'lon'), may hold values from 0.18 to 0.24
- inverse_area: float32 [512, 4096], P('lat', 'lon'), may hold values from 0.7 to 1
- land_sea: int32 [512, 4096], P('lat', 'lon'), may hold values 0 or 1
Outputs:
- ensemble_coefficients: bfloat16 [32, 2, 512, 4096], P(None, None, 'lat', 'lon')
- climate_coefficients: float32 [2, 512, 4096], P(None, 'lat', 'lon')
All inputs are finite; a program needn't handle non-finite values. No bound on the sum of `land_sea` on one device may be relied on, other than what follows from the above.
Results may differ from a plain program's by a relative error of at most 0.001.
Values sent between devices are 32-bit elements; how exact they have to be, the bound alone decides.
No kernel may reach another device: no remote copies, remote signals or barrier semaphores. Data moves between devices by JAX's collectives and lax.ppermute only.
A program may use at most 64 MiB of HBM per device.

v0:
```python
import functools

import jax
import jax.numpy as jnp
import numpy as np
from jax import lax
from jax.experimental import pallas as pl
from jax.experimental.pallas import tpu as pltpu
from jax.sharding import PartitionSpec as P

STEPS = 6
ENSEMBLE_WEIGHT = 0.8
CLIMATE_WEIGHT = 0.6
ROWS = 64
LANES = 128
GROUPS = 9
PHASES = 4
SETS = 3
SPAN = (LANES + 2 * STEPS) // PHASES
VECS = PHASES * SETS
SLOT = 2 * STEPS
EXT = ROWS + 2 * STEPS
TILE = (8, LANES)
AXES = ("lon", "lat")
F32 = jnp.float32
BF16 = jnp.bfloat16
MIB = 1024 * 1024


def tables():
    edge = np.zeros((8, LANES, LANES), np.float32)
    for g in range(8):
        for n in range(STEPS):
            edge[g, LANES - STEPS + n, SLOT * g + n] = 1
            edge[g, n, SLOT * g + STEPS + n] = 1
    into = np.zeros((SETS, LANES, PHASES, LANES), np.float32)
    for k in range(SETS):
        for c in range(LANES):
            into[k, c, (c + STEPS) % PHASES, SPAN * k + (c + STEPS) // PHASES] = 1
    into = into.reshape(SETS * LANES, PHASES * LANES)
    return [jnp.asarray(x, BF16) for x in (edge.reshape(4, 2 * LANES, LANES), into)]


def lanes():
    return lax.broadcasted_iota(jnp.int32, TILE, 1)


def gather(x, index):
    return jnp.take_along_axis(x, index, axis=1)


def dot(a, b, side=0):
    return lax.dot_general(a, b, (((1,), (side,)), ((), ())), preferred_element_type=F32)


def is_odd():
    return lax.rem(lax.axis_index("lat"), 2) == 1


def row_tile(index):
    return pl.ds(pl.multiple_of(index * 16, 16), 16)


def vmem(n):
    return [pl.BlockSpec(memory_space=pltpu.VMEM)] * n


def call(kernel, name, outs, n_in, scratch=(), limit=16, cost=(0, 0), in_specs=None, out_specs=None, aliases=None):
    return pl.pallas_call(
        kernel,
        name=name,
        out_shape=[jax.ShapeDtypeStruct(s, d) for s, d in outs],
        in_specs=in_specs or vmem(n_in),
        out_specs=out_specs or vmem(len(outs)),
        scratch_shapes=list(scratch),
        input_output_aliases=aliases or {},
        compiler_params=pltpu.CompilerParams(vmem_limit_bytes=limit * MIB),
        cost_estimate=pl.CostEstimate(flops=cost[0], bytes_accessed=cost[1], transcendentals=0),
    )


def edges(
    mem, inc, clim, dif, inv, land, table, into, msg_a, msg_b, msg_e, mem_v, src_v, into_v,
    side_rows, inc_v, clim_v, dif_v, inv_v, land_v, table_v, sem,
):
    pairs = [(inc, inc_v), (land, land_v), (clim, clim_v), (dif, dif_v), (inv, inv_v)]
    part = mem.shape[0] // 4
    pairs += [(mem.at[pl.ds(part * n, part)], mem_v.at[pl.ds(part * n, part)]) for n in range(4)]
    pairs += [(table, table_v), (into, into_v)]
    copies = [pltpu.make_async_copy(a, b, sem.at[n]) for n, (a, b) in enumerate(pairs)]
    for copy in copies:
        copy.start()
    odd = is_odd()
    lane = lanes()
    for copy in copies[:5]:
        copy.wait()
    wet = land_v[...].astype(F32)
    for v in range(2):
        masked = inc_v[v] * wet
        src_v[v] = ENSEMBLE_WEIGHT * masked
        src_v[2 + v] = CLIMATE_WEIGHT * (clim_v[v] * masked)
    src_v[4] = dif_v[...] * wet
    src_v[5] = inv_v[...]
    zero = jnp.zeros(TILE, F32)

    for side in range(2):
        cut = slice(8 * side, 8 * side + 8)
        rows = pl.ds(56 * side, 8)
        pattern = jnp.stack([src_v[0, rows], src_v[1, rows]] * 4)
        for g in range(GROUPS):
            if g < 8:
                if side == 0 and g % 2 == 0:
                    copies[5 + g // 2].wait()
                block = mem_v[8 * g : 8 * g + 8, pl.ds(48 * side, 16), :].astype(F32)[:, cut] * pattern
            else:
                block = jnp.stack([src_v[2 + n, rows] for n in range(4)] + [zero] * 4)
            block = jnp.swapaxes(block, 0, 1)
            for k in range(STEPS):
                side_rows[side, k, g] = block[7 - k if side else k]
    a_side = jnp.where(odd, 0, 1)
    msg_a[...] = side_rows[a_side]
    msg_b[...] = side_rows[1 - a_side]

    n = lax.rem(lane, SLOT)
    column = jnp.where(n < STEPS, LANES - STEPS + n, n - STEPS)
    ensemble = lane < 8 * SLOT
    climate = (lane >= 8 * SLOT) & (lane < 9 * SLOT)
    copies[9].wait()
    acc = None
    for q in range(4):
        pair = [mem_v[16 * q + 8 * j : 16 * q + 8 * j + 8].reshape(8 * ROWS, LANES) for j in range(2)]
        x = dot(jnp.concatenate(pair, axis=1), table_v[q])
        acc = x if acc is None else acc + x
    acc = acc.reshape(8, ROWS, LANES)
    for m in range(ROWS // 8):
        cut = slice(8 * m, 8 * m + 8)
        ends = [gather(src_v[f, cut], column) for f in range(6)] + [zero] * 4
        block = [
            jnp.where(ensemble, acc[f, cut] * ends[f % 2], jnp.where(climate, ends[2 + f], 0.0)) for f in range(8)
        ]
        block = jnp.swapaxes(jnp.stack(block), 0, 1)
        for e in range(8):
            r = 8 * m + e
            msg_e[jnp.where(odd, r, ROWS - 1 - r)] = block[e]
    copies[10].wait()


def layout(fold=False):
    lane = lanes()
    part = lane // SPAN
    out = []
    for p in range(PHASES):
        e = PHASES * (lane - SPAN * part) + p
        west, east = e < STEPS, e >= LANES + STEPS
        column = jnp.clip(e - STEPS, 0, LANES - 1)
        n = jnp.where(west, e, jnp.clip(e - LANES, 0, SLOT - 1))
        column = jnp.where(fold, LANES - 1 - column, column)
        n = jnp.where(fold, SLOT - 1 - n, n)
        out.append((column, west | east, jnp.minimum(SLOT * part + n, LANES - 1 - 2 * SETS * SLOT)))
    return out


def spread(mem, src, table, state):
    odd = is_odd()
    part = lanes() // SPAN
    places = layout()

    def tile(m, _):
        rows = row_tile(m)
        for t in range(SETS):
            n = 3 if t < 2 else 2
            lhs = [mem[pl.ds(8 * (3 * t + k), 8), rows, :].reshape(8 * 16, LANES) for k in range(n)]
            out = dot(jnp.concatenate(lhs, axis=1), table[: n * LANES, :]).reshape(8, 16, PHASES * LANES)
            for p in range(PHASES):
                column, halo, _ = places[p]
                for h in range(2):
                    cut = slice(8 * h, 8 * h + 8)
                    half = pl.ds(pl.multiple_of(m * 16 + 8 * h, 8), 8)
                    weights = [gather(src[v, half], column) for v in range(2)]
                    block = [out[f, cut, LANES * p : LANES * p + LANES] * weights[f % 2] for f in range(8)]
                    if t == 2:
                        own = (part == 2) & ~halo
                        for f in range(4):
                            block[f] = jnp.where(own, gather(src[2 + f, half], column), block[f])
                    block = jnp.swapaxes(jnp.stack(block), 0, 1)
                    for e in range(8):
                        r = m * 16 + 8 * h + e
                        state[jnp.where(odd, r, ROWS - 1 - r), PHASES * t + p] = block[e]
        return 0

    lax.fori_loop(0, ROWS // 16, tile, 0)


def corner(p1, p2, halo, cor_a, cor_b):
    west_first = lax.rem(lax.axis_index("lon"), 2) == 1
    from_first = (lax.rem(lanes(), SLOT) < STEPS) == west_first

    def row(r, _):
        halo[r] = jnp.where(from_first, p1[r], p2[r])
        return 0

    lax.fori_loop(0, ROWS, row, 0, unroll=8)
    for k in range(STEPS):
        cor_a[k] = halo[k]
        cor_b[k] = halo[ROWS - 1 - k]


def join(state, r, cor, main, places):
    part = lanes() // SPAN
    for t in range(SETS):
        for p in range(PHASES):
            column, is_halo, place = places[p]
            x = gather(cor, place + SETS * SLOT * t)
            if callable(main):
                own = main(PHASES * t + p)
            else:
                own = gather(main[3 * t], column)
                for k in (1, 2):
                    own = jnp.where(part == k, gather(main[3 * t + k], column), own)
            state[r, PHASES * t + p] = jnp.where(is_halo, x, own)


def flat(ref):
    n = 1
    for d in ref.shape[:-1]:
        n *= d
    return ref.reshape((n, LANES))


def east(x):
    return [x[p + 1] if p < PHASES - 1 else pltpu.roll(x[0], LANES - 1, 1) for p in range(PHASES)]


def west(x):
    return [x[p - 1] if p else pltpu.roll(x[PHASES - 1], 1, 1) for p in range(PHASES)]


def weigh(state, count, ground, dense, coef):
    lane = lanes()
    index = 2 * SPAN + lane - SPAN * (lane // SPAN)
    rows = flat(state)
    blocks = -(-count // 8)
    for b in range(blocks):
        for p in range(PHASES):
            for w in range(2):
                start = (8 * b * VECS + 2 * PHASES + p) * 8 + 2 + w
                x = rows[pl.ds(start, 8, stride=8 * VECS), :]
                ground[PHASES * w + p, 8 * b + 8 : 8 * b + 16, :] = gather(x, index)
    for b in range(blocks):
        con, con_a, con_b, inv, inv_a, inv_b = [
            [ground[PHASES * w + p, 8 * b + 8 + d : 8 * b + 16 + d, :] for p in range(PHASES)]
            for w in range(2)
            for d in (0, 1, -1)
        ]
        f_e = [jnp.sqrt(x * y) for x, y in zip(con, east(con))]
        f_w = west(f_e)
        i_e, i_w = east(inv), west(inv)
        for p in range(PHASES):
            f_a, f_b = jnp.sqrt(con[p] * con_a[p]), jnp.sqrt(con[p] * con_b[p])
            out = (
                1.0 - inv[p] * ((f_e[p] + f_w[p]) + (f_a + f_b)),
                f_e[p] * i_e[p],
                f_w[p] * i_w[p],
                f_a * inv_a[p],
                f_b * inv_b[p],
            )
            for n in range(5):
                dense[5 * p + n, 8 * b : 8 * b + 8, :] = out[n]

    def expand(r, _):
        for n in range(5 * PHASES):
            coef[r, n] = jnp.broadcast_to(dense[n, pl.ds(r, 1), :], TILE)
        return 0

    lax.fori_loop(1, count - 1, expand, 0, unroll=4)


def advance(row, before, after, coef, c):
    weights = [[coef[c, 5 * p + n] for n in range(5)] for p in range(PHASES)]
    out = []
    for t in range(SETS):
        x = [row(PHASES * t + p) for p in range(PHASES)]
        x_e, x_w = east(x), west(x)
        for p in range(PHASES):
            c0, c_e, c_w, c_a, c_b = weights[p]
            q = PHASES * t + p
            out.append((c0 * x[p] + c_e * x_e[p]) + (c_w * x_w[p] + (c_a * after(q) + c_b * before(q))))
    return out


def finish(row, odd, table, ens_out, clim_out, rows):
    lane = lanes()
    index = 2 * SPAN + (lane + STEPS) // PHASES
    phase = lax.rem(lane + STEPS, PHASES)
    for t in range(SETS):
        blocks = []
        for p in range(PHASES):
            halves = []
            for h in range(2):
                x = jnp.stack([row(8 * h + e, PHASES * t + p) for e in range(8)])
                halves.append(jnp.swapaxes(x, 0, 1))
            blocks.append(jnp.concatenate(halves, axis=1))
        if t == 2:
            for v in range(2):
                halves = []
                for h in range(2):
                    cut = slice(8 * h, 8 * h + 8)
                    x = gather(blocks[0][v, cut], index)
                    for p in range(1, PHASES):
                        x = jnp.where(phase == p, gather(blocks[p][v, cut], index), x)
                    halves.append(x)
                clim_out[v, rows, :] = jnp.concatenate(halves, axis=0)
        lhs = jnp.concatenate([x.astype(BF16).reshape(8 * 16, LANES) for x in blocks], axis=1)
        out = dot(lhs, table[...], 1).astype(BF16)
        for k in range(3 if t < 2 else 2):
            ens_out[pl.ds(8 * (3 * t + k), 8), rows, :] = out[:, LANES * k : LANES * k + LANES].reshape(8, 16, LANES)


NEAR = STEPS + 1
FIN = 16 - STEPS


def main(own, halo, msg_a, cor_a, table, ens, clim, near, kept, fin, first, second, ground, dense, coef):
    odd = is_odd()
    places = layout()

    def take(r, _):
        join(first, r + STEPS, halo[r], lambda q: own[r, q], places)
        return 0

    lax.fori_loop(0, ROWS, take, 0, unroll=16)
    for k in range(STEPS):
        join(first, STEPS - 1 - k, cor_a[k], [msg_a[k, g] for g in range(GROUPS)], places)
    end = STEPS + ROWS

    weigh(first, end, ground, dense, coef)
    for n in range(NEAR):
        near[n] = first[end - NEAR + n]

    for s in range(STEPS):
        src, dst = (first, second) if s % 2 == 0 else (second, first)
        if s:
            kept[s - 1, 0] = src[end - s - 2]
            kept[s - 1, 1] = src[end - s - 1]

        def step(r, _, src=src, dst=dst):
            out = advance(lambda q: src[r, q], lambda q: src[r - 1, q], lambda q: src[r + 1, q], coef, r)
            for q in range(VECS):
                dst[r, q] = out[q]
            return 0

        lax.fori_loop(s + 1, end - s - 1, step, 0, unroll=8)
    for n in range(FIN):
        fin[n] = first[end - 16 + n]

    def tile(m, _):
        src = jnp.where(odd, m, ROWS // 16 - 1 - m)

        def row(n, q):
            r = src * 16 + n
            return first[STEPS + jnp.where(odd, r, ROWS - 1 - r), q]

        finish(row, odd, table, ens, clim, row_tile(src))
        return 0

    lax.fori_loop(0, ROWS // 16 - 1, tile, 0)


def tail(near, kept, fin, msg_b, cor_b, table, ens_in, clim_in, ens, clim, one, two, ground, dense, coef, ens_rows, clim_rows, sem):
    del ens_in, clim_in
    odd = is_odd()
    fold = lax.axis_index("lat") == lax.axis_size("lat") - 1
    places = layout(fold)
    for n in range(NEAR):
        one[n] = near[n]
    for k in range(STEPS):
        join(one, NEAR + k, cor_b[k], [msg_b[k, g] for g in range(GROUPS)], places)
    weigh(one, NEAR + STEPS, ground, dense, coef)
    for s in range(STEPS):
        src, dst = (one, two) if s % 2 == 0 else (two, one)
        lo = NEAR - 1 - s
        if s:
            src[lo - 1] = kept[s - 1, 0]
            src[lo] = kept[s - 1, 1]
        for n in range(lo, lo + STEPS):
            out = advance(lambda q: src[n, q], lambda q: src[n - 1, q], lambda q: src[n + 1, q], coef, n)
            for q in range(VECS):
                dst[n, q] = out[q]
    for n in range(FIN):
        two[n] = fin[n]
    for n in range(STEPS):
        two[FIN + n] = one[1 + n]

    def row(n, q):
        return two[jnp.where(odd, n, 15 - n), q]

    finish(row, odd, table, ens_rows, clim_rows, pl.ds(0, 16))
    rows = row_tile(jnp.where(odd, ROWS // 16 - 1, 0))
    copies = [
        pltpu.make_async_copy(ens_rows, ens.at[:, rows, :], sem.at[0]),
        pltpu.make_async_copy(clim_rows, clim.at[:, rows, :], sem.at[1]),
    ]
    for copy in copies:
        copy.start()
    for copy in copies:
        copy.wait()


def body(n_lon, n_lat, increment, members, climate_spread, diffusivity, inverse_area, land_sea):
    def place(i, l):
        return i % n_lon * n_lat + l

    def route(target):
        pairs = [(i, l, target(i, l)) for i in range(n_lon) for l in range(n_lat)]
        return [(place(i, l), place(*t)) for i, l, t in pairs if t is not None]

    def pair_b(i, l):
        if l == n_lat - 1:
            return (n_lon - 1 - i, l)
        return None if l == 0 else (i, l + 1 if l % 2 else l - 1)

    route_a = route(lambda i, l: (i, l ^ 1))
    route_b = route(pair_b)
    route_1 = route(lambda i, l: (i ^ 1, l))
    route_2 = route(lambda i, l: ((i + (1 if i % 2 else -1)) % n_lon, l))
    table_edge, table_in = tables()
    count = members.shape[0] * 2
    arrays = (members.reshape(count, ROWS, LANES), increment, climate_spread, diffusivity, inverse_area, land_sea)
    side = (STEPS, GROUPS, *TILE)
    hbm = [pl.BlockSpec(memory_space=pltpu.HBM)] * 8
    two = (2, ROWS, LANES)
    msg_a, msg_b, msg_e, mem_v, src_v, into_v = call(
        edges,
        "edges",
        [(side, F32), (side, F32), ((ROWS, *TILE), F32)]
        + [((count, ROWS, LANES), BF16), ((6, ROWS, LANES), F32), (table_in.shape, BF16)],
        8,
        [pltpu.VMEM((2, *side), F32), pltpu.VMEM(two, F32), pltpu.VMEM(two, F32)]
        + [pltpu.VMEM((ROWS, LANES), d) for d in (F32, F32, jnp.int32)]
        + [pltpu.VMEM(table_edge.shape, BF16), pltpu.SemaphoreType.DMA((11,))],
        limit=12,
        in_specs=hbm,
    )(*[pltpu.with_memory_space_constraint(x, pltpu.HBM) for x in (*arrays, table_edge, table_in)])
    got_b = lax.ppermute(msg_b, AXES, route_b)
    got_a = lax.ppermute(msg_a, AXES, route_a)
    p1 = lax.ppermute(msg_e, AXES, route_1)
    p2 = lax.ppermute(msg_e, AXES, route_2)
    (own,) = call(spread, "spread", [((ROWS, VECS, *TILE), F32)], 3, limit=12)(mem_v, src_v, into_v)
    p1, p2, own = lax.optimization_barrier((p1, p2, own))
    halo, cor_a, cor_b = call(
        corner, "corner", [((ROWS, *TILE), F32), ((STEPS, *TILE), F32), ((STEPS, *TILE), F32)], 2, limit=4
    )(p1, p2)
    cor_a = lax.ppermute(cor_a, AXES, route_a)
    cor_b = lax.ppermute(cor_b, AXES, route_b)
    full = [((count, ROWS, LANES), BF16), ((2, ROWS, LANES), F32)]
    vecs = (VECS, *TILE)
    ens, clim, near, kept, fin = call(
        main,
        "main",
        full + [((NEAR, *vecs), F32), ((STEPS - 1, 2, *vecs), F32), ((FIN, *vecs), F32)],
        5,
        [pltpu.VMEM((EXT, *vecs), F32)] * 2
        + [pltpu.VMEM((n, EXT + 20, LANES), F32) for n in (2 * PHASES, 5 * PHASES)]
        + [pltpu.VMEM((EXT, 5 * PHASES, *TILE), F32)],
        limit=32,
    )(own, halo, got_a, cor_a, into_v)
    anywhere = [pl.BlockSpec(memory_space=pl.ANY)] * 2
    ens, clim = call(
        tail,
        "tail",
        full,
        8,
        [pltpu.VMEM((16, *vecs), F32)] * 2
        + [pltpu.VMEM((n, 32, LANES), F32) for n in (2 * PHASES, 5 * PHASES)]
        + [pltpu.VMEM((16, 5 * PHASES, *TILE), F32)]
        + [pltpu.VMEM((count, 16, LANES), BF16), pltpu.VMEM((2, 16, LANES), F32), pltpu.SemaphoreType.DMA((2,))],
        limit=12,
        in_specs=vmem(6) + anywhere,
        out_specs=anywhere,
        aliases={6: 0, 7: 1},
    )(near, kept, fin, got_b, cor_b, into_v, ens, clim)
    return ens.reshape(members.shape), clim


def solution(mesh):
    return jax.shard_map(
        functools.partial(body, mesh.shape["lon"], mesh.shape["lat"]),
        mesh=mesh,
        in_specs=(
            P(None, "lat", "lon"),
            P(None, None, "lat", "lon"),
            P(None, "lat", "lon"),
            P("lat", "lon"),
            P("lat", "lon"),
            P("lat", "lon"),
        ),
        out_specs=(P(None, None, "lat", "lon"), P(None, "lat", "lon")),
        check_vma=False,
    )
```

profile of v0, /device:TPU:29, one launch (start us, length us, event | category | flops | bytes accessed | tf_op | source)
XLA Modules:
  0.0 39.1 jit_solution(11280406544970140228)
XLA Ops:
  0.6 2.0 %edges.1 = (f32[6,9,8,128]{3,2,1,0:T(8,128)S(1)}, f32[6,9,8,128]{3,2,1,0:T(8,128)S(1)}, f32[64,8,128]{2,1,0:T(8,128)S(1)}, bf16[64,64,128]{2,1,0:T(8,128)(2,1)S(...) custom-call(bf16[64,64,128]{2,1,0:T(8,128)(2,1)} %bitcast.3, f32[2,64,128]{2,1,0:T(8,128)} %inc.1, ...), custom_call_target="tpu_custom_call" | custom-call | tf_op jit(solution)/shard_map/edges/pallas_call | solution.py:432
  2.6 1.6 %collective-permute-start.1 = (f32[64,8,128]{2,1,0:T(8,128)S(1)}, f32[64,8,128]{2,1,0:T(8,128)S(1)}, u32[]{:S(2)}, u32[]{:S(2)}) collective-permute-start(f32[64,8,128]{2,1,0:T(8,128)S(1)} %get-tuple-element.21), channel_id=1, source_target_pairs={{0,248},{1,249},{2,250},{3,251},{4,252},{5,253},{6,254},{7,255},{8... | collective-permute-start | bytes 786440 | tf_op jit(solution)/shard_map/ppermute | solution.py:447
  4.2 5.1 %collective-permute-start = (f32[64,8,128]{2,1,0:T(8,128)S(1)}, f32[64,8,128]{2,1,0:T(8,128)S(1)}, u32[]{:S(2)}, u32[]{:S(2)}) collective-permute-start(f32[64,8,128]{2,1,0:T(8,128)S(1)} %get-tuple-element.21), channel_id=1, source_target_pairs={{0,8},{1,9},{2,10},{3,11},{4,12},{5,13},{6,14},{7,15},{8,0},{9,1},... | collective-permute-start | bytes 786440 | tf_op jit(solution)/shard_map/ppermute | solution.py:446
  9.3 0.5 %collective-permute-start.2 = (f32[6,9,8,128]{3,2,1,0:T(8,128)S(1)}, f32[6,9,8,128]{3,2,1,0:T(8,128)S(1)}, u32[]{:S(2)}, u32[]{:S(2)}) collective-permute-start(f32[6,9,8,128]{3,2,1,0:T(8,128)S(1)} %get-tuple-element.29), channel_id=1, source_target_pairs={{0,1},{1,0},{2,3},{3,2},{4,5},{5,4},{6,7},{7,6},{8,9},{9,8},{10,11... | collective-permute-start | bytes 663560 | tf_op jit(solution)/shard_map/ppermute | solution.py:445
  9.8 2.6 %collective-permute-start.4 = (f32[6,9,8,128]{3,2,1,0:T(8,128)S(1)}, f32[6,9,8,128]{3,2,1,0:T(8,128)S(1)}, u32[]{:S(2)}, u32[]{:S(2)}) collective-permute-start(f32[6,9,8,128]{3,2,1,0:T(8,128)S(1)} %get-tuple-element.34), channel_id=1, source_target_pairs={{1,2},{2,1},{3,4},{4,3},{5,6},{6,5},{7,255},{9,10},{10,9},{11,12},... | collective-permute-start | bytes 663560 | tf_op jit(solution)/shard_map/ppermute | solution.py:444
  12.4 1.7 %spread.1.own = f32[64,12,8,128]{3,2,1,0:T(8,128)S(1)} custom-call(bf16[64,64,128]{2,1,0:T(8,128)(2,1)S(1)} %get-tuple-element.22.mem, f32[6,64,128]{2,1,0:T(8,128)S(1)} %get-tuple-element.23.src, bf16[384,512]{1,0:T(8,128)(2,1)S(1)} %get-tuple-element.24.table), custom_call_target="tpu_custom_call" | custom-call | tf_op jit(solution)/shard_map/spread/pallas_call | solution.py:448
  14.2 0.0 collective-permute-done.1.p2
  14.2 0.0 collective-permute-done.p1
  14.2 0.1 corner.1
  14.3 0.4 collective-permute-start.3
  14.7 8.0 %collective-permute-start.5 = (f32[6,8,128]{2,1,0:T(8,128)S(1)}, f32[6,8,128]{2,1,0:T(8,128)S(1)}, u32[]{:S(2)}, u32[]{:S(2)}) collective-permute-start(f32[6,8,128]{2,1,0:T(8,128)S(1)} %get-tuple-element.35), channel_id=1, source_target_pairs={{1,2},{2,1},{3,4},{4,3},{5,6},{6,5},{7,255},{9,10},{10,9},{11,12},... | collective-permute-start | bytes 73736 | tf_op jit(solution)/shard_map/ppermute | solution.py:454
  22.7 0.0 collective-permute-done.2.msg_a
  22.7 0.0 collective-permute-done.3.cor_a
  22.7 13.4 %main.1 = (bf16[64,64,128]{2,1,0:T(8,128)(2,1)}, f32[2,64,128]{2,1,0:T(8,128)}, f32[7,12,8,128]{3,2,1,0:T(8,128)S(1)}, f32[5,2,12,8,128]{4,3,2,1,0:T(8,128)S(1)}, f32[10,12,8,128]{3,2,1,0:T(8,128)S(1)}) custom-call(f32[64,12,8,128]{3,2,1,0:T(8,128)S(1)} %spread.1.own, f32[64,8,128]{2,1,0:T(8,128)S(1)} %get-tuple-element.28.halo, ...), custom_call_target="tpu_custom_call" | custom-call | tf_op jit(solution)/shard_map/main/pallas_call | solution.py:457
  36.1 0.0 collective-permute-done.4.msg_b
  36.1 0.0 collective-permute-done.5.cor_b
  36.1 3.0 %tail.1 = (bf16[64,64,128]{2,1,0:T(8,128)(2,1)}, f32[2,64,128]{2,1,0:T(8,128)}) custom-call(f32[7,12,8,128]{3,2,1,0:T(8,128)S(1)} %get-tuple-element.31.near, f32[5,2,12,8,128]{4,3,2,1,0:T(8,128)S(1)} %get-tuple-element.32.kept, f32[10,12,8,128]{3,2,1,0:T(8,128)S(1)} %get-tuple-element.33.fin, ...), custom_call_target="tpu_custom_call", output_to_operand_aliasing={{0}: (6, {}), {1}: (7, {})} | custom-call | tf_op jit(solution)/shard_map/tail/pallas_call | solution.py:468
Async XLA Ops:
  2.6 11.5 %collective-permute-start.1 = (f32[64,8,128]{2,1,0:T(8,128)S(1)}, f32[64,8,128]{2,1,0:T(8,128)S(1)}, u32[]{:S(2)}, u32[]{:S(2)}) collective-permute-start(f32[64,8,128]{2,1,0:T(8,128)S(1)} %get-tuple-element.21), channel_id=1, source_target_pairs={{0,248},{1,249},{2,250},{3,251},{4,252},{5,253},{6,254},{7,255},{8... | collective-permute-start | bytes 786440 | tf_op jit(solution)/shard_map/ppermute | solution.py:447
  4.2 10.0 %collective-permute-start = (f32[64,8,128]{2,1,0:T(8,128)S(1)}, f32[64,8,128]{2,1,0:T(8,128)S(1)}, u32[]{:S(2)}, u32[]{:S(2)}) collective-permute-start(f32[64,8,128]{2,1,0:T(8,128)S(1)} %get-tuple-element.21), channel_id=1, source_target_pairs={{0,8},{1,9},{2,10},{3,11},{4,12},{5,13},{6,14},{7,15},{8,0},{9,1},... | collective-permute-start | bytes 786440 | tf_op jit(solution)/shard_map/ppermute | solution.py:446
  9.3 13.3 %collective-permute-start.2 = (f32[6,9,8,128]{3,2,1,0:T(8,128)S(1)}, f32[6,9,8,128]{3,2,1,0:T(8,128)S(1)}, u32[]{:S(2)}, u32[]{:S(2)}) collective-permute-start(f32[6,9,8,128]{3,2,1,0:T(8,128)S(1)} %get-tuple-element.29), channel_id=1, source_target_pairs={{0,1},{1,0},{2,3},{3,2},{4,5},{5,4},{6,7},{7,6},{8,9},{9,8},{10,11... | collective-permute-start | bytes 663560 | tf_op jit(solution)/shard_map/ppermute | solution.py:445
  9.8 26.3 %collective-permute-start.4 = (f32[6,9,8,128]{3,2,1,0:T(8,128)S(1)}, f32[6,9,8,128]{3,2,1,0:T(8,128)S(1)}, u32[]{:S(2)}, u32[]{:S(2)}) collective-permute-start(f32[6,9,8,128]{3,2,1,0:T(8,128)S(1)} %get-tuple-element.34), channel_id=1, source_target_pairs={{1,2},{2,1},{3,4},{4,3},{5,6},{6,5},{7,255},{9,10},{10,9},{11,12},... | collective-permute-start | bytes 663560 | tf_op jit(solution)/shard_map/ppermute | solution.py:444
  14.3 8.4 %collective-permute-start.3 = (f32[6,8,128]{2,1,0:T(8,128)S(1)}, f32[6,8,128]{2,1,0:T(8,128)S(1)}, u32[]{:S(2)}, u32[]{:S(2)}) collective-permute-start(f32[6,8,128]{2,1,0:T(8,128)S(1)} %get-tuple-element.30), channel_id=1, source_target_pairs={{0,1},{1,0},{2,3},{3,2},{4,5},{5,4},{6,7},{7,6},{8,9},{9,8},{10,11... | collective-permute-start | bytes 73736 | tf_op jit(solution)/shard_map/ppermute | solution.py:453
  14.7 21.4 %collective-permute-start.5 = (f32[6,8,128]{2,1,0:T(8,128)S(1)}, f32[6,8,128]{2,1,0:T(8,128)S(1)}, u32[]{:S(2)}, u32[]{:S(2)}) collective-permute-start(f32[6,8,128]{2,1,0:T(8,128)S(1)} %get-tuple-element.35), channel_id=1, source_target_pairs={{1,2},{2,1},{3,4},{4,3},{5,6},{6,5},{7,255},{9,10},{10,9},{11,12},... | collective-permute-start | bytes 73736 | tf_op jit(solution)/shard_map/ppermute | solution.py:454
where the time goes:
time: 39.2 us; the launch traced here: 39.1 us
  Pallas kernels  20.2 us (52%)
  starting transfers between devices  18.1 us (46%)
  between operations  0.7 us (2%)
    pallas_call x1, Pallas kernels, body(): call(main, 'main', full + [((NEAR, *vecs), F32), ((STEPS - 1, 2, *vecs),...  13.4 us
    ppermute x1, starting transfers between devices, body(): cor_b = lax.ppermute(cor_b, AXES, route_b)  7.99 us
    ppermute x1, starting transfers between devices, body(): p1 = lax.ppermute(msg_e, AXES, route_1)  5.13 us
    pallas_call x1, Pallas kernels, body(): call(tail, 'tail', full, 8, [pltpu.VMEM((16, *vecs), F32)] * 2 + [pltpu.V...  2.99 us
    ppermute x1, starting transfers between devices, body(): got_b = lax.ppermute(msg_b, AXES, route_b)  2.61 us
    pallas_call x1, Pallas kernels, body(): call(edges, 'edges', [(side, F32), (side, F32), ((ROWS, *TILE), F32)] + [...  2 us
    pallas_call x1, Pallas kernels, body(): call(spread, 'spread', [((ROWS, VECS, *TILE), F32)], 3, limit=12)  1.75 us
    ppermute x1, starting transfers between devices, body(): p2 = lax.ppermute(msg_e, AXES, route_2)  1.57 us
  transfers between devices with their start and end apart: 6, of which 0 were waited for; matrix products, arithmetic and copies ran while one was open for 0% of the time, Pallas kernels for 39%

commit v1 on v0

--- a/solution.py
+++ b/solution.py
@@ -18,7 +18,7 @@
 SETS = 3
 SPAN = (LANES + 2 * STEPS) // PHASES
 VECS = PHASES * SETS
-SLOT = 2 * STEPS
+HALF = LANES // 2
 EXT = ROWS + 2 * STEPS
 TILE = (8, LANES)
 AXES = ("lon", "lat")
@@ -31,14 +31,20 @@
     edge = np.zeros((8, LANES, LANES), np.float32)
     for g in range(8):
         for n in range(STEPS):
-            edge[g, LANES - STEPS + n, SLOT * g + n] = 1
-            edge[g, n, SLOT * g + STEPS + n] = 1
+            edge[g, LANES - STEPS + n, STEPS * g + n] = 1
+            edge[g, n, HALF + STEPS * g + n] = 1
     into = np.zeros((SETS, LANES, PHASES, LANES), np.float32)
     for k in range(SETS):
         for c in range(LANES):
             into[k, c, (c + STEPS) % PHASES, SPAN * k + (c + STEPS) // PHASES] = 1
     into = into.reshape(SETS * LANES, PHASES * LANES)
-    return [jnp.asarray(x, BF16) for x in (edge.reshape(4, 2 * LANES, LANES), into)]
+    halo = np.zeros((SETS, LANES, PHASES, LANES), np.float32)
+    for g in range(GROUPS):
+        for n in range(STEPS):
+            for first, e in ((0, n), (HALF, LANES + STEPS + n)):
+                halo[g // SETS, first + STEPS * g + n, e % PHASES, SPAN * (g % SETS) + e // PHASES] = 1
+    halo = halo.reshape(SETS, LANES, PHASES * LANES)
+    return [jnp.asarray(x, BF16) for x in (edge.reshape(4, 2 * LANES, LANES), into, halo)]
 
 
 def lanes():
@@ -65,7 +71,7 @@
     return [pl.BlockSpec(memory_space=pltpu.VMEM)] * n
 
 
-def call(kernel, name, outs, n_in, scratch=(), limit=16, cost=(0, 0), in_specs=None, out_specs=None, aliases=None):
+def call(kernel, name, outs, n_in, scratch=(), limit=16, cost=(0, 0), in_specs=None, out_specs=None):
     return pl.pallas_call(
         kernel,
         name=name,
@@ -73,20 +79,19 @@
         in_specs=in_specs or vmem(n_in),
         out_specs=out_specs or vmem(len(outs)),
         scratch_shapes=list(scratch),
-        input_output_aliases=aliases or {},
         compiler_params=pltpu.CompilerParams(vmem_limit_bytes=limit * MIB),
         cost_estimate=pl.CostEstimate(flops=cost[0], bytes_accessed=cost[1], transcendentals=0),
     )
 
 
 def edges(
-    mem, inc, clim, dif, inv, land, table, into, msg_a, msg_b, msg_e, mem_v, src_v, into_v,
-    side_rows, inc_v, clim_v, dif_v, inv_v, land_v, table_v, sem,
+    mem, inc, clim, dif, inv, land, table, into, tab_h, msg_a, msg_b, msg_1, msg_2, mem_v, src_v, into_v, tab_h_v,
+    side_rows, rim, inc_v, clim_v, dif_v, inv_v, land_v, table_v, sem,
 ):
     pairs = [(inc, inc_v), (land, land_v), (clim, clim_v), (dif, dif_v), (inv, inv_v)]
     part = mem.shape[0] // 4
     pairs += [(mem.at[pl.ds(part * n, part)], mem_v.at[pl.ds(part * n, part)]) for n in range(4)]
-    pairs += [(table, table_v), (into, into_v)]
+    pairs += [(table, table_v), (into, into_v), (tab_h, tab_h_v)]
     copies = [pltpu.make_async_copy(a, b, sem.at[n]) for n, (a, b) in enumerate(pairs)]
     for copy in copies:
         copy.start()
@@ -121,10 +126,8 @@
     msg_a[...] = side_rows[a_side]
     msg_b[...] = side_rows[1 - a_side]
 
-    n = lax.rem(lane, SLOT)
-    column = jnp.where(n < STEPS, LANES - STEPS + n, n - STEPS)
-    ensemble = lane < 8 * SLOT
-    climate = (lane >= 8 * SLOT) & (lane < 9 * SLOT)
+    column = rim_column()
+    ensemble = lax.rem(lane, HALF) < 8 * STEPS
     copies[9].wait()
     acc = None
     for q in range(4):
@@ -136,13 +139,28 @@
         cut = slice(8 * m, 8 * m + 8)
         ends = [gather(src_v[f, cut], column) for f in range(6)] + [zero] * 4
         block = [
-            jnp.where(ensemble, acc[f, cut] * ends[f % 2], jnp.where(climate, ends[2 + f], 0.0)) for f in range(8)
+            jnp.where(ensemble, acc[f, cut] * ends[f % 2], ends[2 + f]) for f in range(8)
         ]
         block = jnp.swapaxes(jnp.stack(block), 0, 1)
         for e in range(8):
             r = 8 * m + e
-            msg_e[jnp.where(odd, r, ROWS - 1 - r)] = block[e]
-    copies[10].wait()
+            rim[jnp.where(odd, r, ROWS - 1 - r)] = block[e]
+    first_east = lax.rem(lax.axis_index("lon"), 2) == 0
+    low = lane < HALF
+    for r in range(ROWS // 2):
+        a, b = rim[r], rim[r + ROWS // 2]
+        east_two = jnp.where(low, a, pltpu.roll(b, HALF, 1))
+        west_two = jnp.where(low, pltpu.roll(a, HALF, 1), b)
+        msg_1[r] = jnp.where(first_east, east_two, west_two)
+        msg_2[r] = jnp.where(first_east, west_two, east_two)
+    for copy in copies[10:]:
+        copy.wait()
+
+
+def rim_column():
+    lane = lanes()
+    n = lax.rem(lax.rem(lane, HALF), STEPS)
+    return jnp.where(lane < HALF, LANES - STEPS + n, n)
 
 
 def layout(fold=False):
@@ -153,10 +171,9 @@
         e = PHASES * (lane - SPAN * part) + p
         west, east = e < STEPS, e >= LANES + STEPS
         column = jnp.clip(e - STEPS, 0, LANES - 1)
-        n = jnp.where(west, e, jnp.clip(e - LANES, 0, SLOT - 1))
         column = jnp.where(fold, LANES - 1 - column, column)
-        n = jnp.where(fold, SLOT - 1 - n, n)
-        out.append((column, west | east, jnp.minimum(SLOT * part + n, LANES - 1 - 2 * SETS * SLOT)))
+        place = STEPS * part + jnp.where(west, e, HALF + jnp.clip(e - LANES - STEPS, 0, STEPS - 1))
+        out.append((column, west | east, jnp.minimum(place, LANES - 1 - 2 * SETS * STEPS)))
     return out
 
 
@@ -191,18 +208,21 @@
     lax.fori_loop(0, ROWS // 16, tile, 0)
 
 
-def corner(p1, p2, halo, cor_a, cor_b):
-    west_first = lax.rem(lax.axis_index("lon"), 2) == 1
-    from_first = (lax.rem(lanes(), SLOT) < STEPS) == west_first
-
-    def row(r, _):
-        halo[r] = jnp.where(from_first, p1[r], p2[r])
-        return 0
-
-    lax.fori_loop(0, ROWS, row, 0, unroll=8)
-    for k in range(STEPS):
-        cor_a[k] = halo[k]
-        cor_b[k] = halo[ROWS - 1 - k]
+def rim_of_halo(msg_a, msg_b, rim):
+    fold = lax.axis_index("lat") == lax.axis_size("lat") - 1
+    group = lax.rem(lanes(), HALF) // STEPS
+    column = rim_column()
+    for side, msg in enumerate((msg_a, msg_b)):
+        index = jnp.where(fold, LANES - 1 - column, column) if side else column
+        for k in range(STEPS):
+            acc = gather(msg[k, 0], index)
+            for g in range(1, GROUPS):
+                acc = jnp.where(group == g, gather(msg[k, g], index), acc)
+            rim[side, k] = acc
+
+
+def west_is_first():
+    return lax.rem(lax.axis_index("lon"), 2) == 1
 
 
 def join(state, r, cor, main, places):
@@ -210,13 +230,10 @@
     for t in range(SETS):
         for p in range(PHASES):
             column, is_halo, place = places[p]
-            x = gather(cor, place + SETS * SLOT * t)
-            if callable(main):
-                own = main(PHASES * t + p)
-            else:
-                own = gather(main[3 * t], column)
-                for k in (1, 2):
-                    own = jnp.where(part == k, gather(main[3 * t + k], column), own)
+            x = gather(cor, place + SETS * STEPS * t)
+            own = gather(main[3 * t], column)
+            for k in (1, 2):
+                own = jnp.where(part == k, gather(main[3 * t + k], column), own)
             state[r, PHASES * t + p] = jnp.where(is_halo, x, own)
 
 
@@ -235,7 +252,7 @@
     return [x[p - 1] if p else pltpu.roll(x[PHASES - 1], 1, 1) for p in range(PHASES)]
 
 
-def weigh(state, count, ground, dense, coef):
+def weigh(state, count, lo, hi, ground, dense, coef, unroll):
     lane = lanes()
     index = 2 * SPAN + lane - SPAN * (lane // SPAN)
     rows = flat(state)
@@ -272,7 +289,7 @@
             coef[r, n] = jnp.broadcast_to(dense[n, pl.ds(r, 1), :], TILE)
         return 0
 
-    lax.fori_loop(1, count - 1, expand, 0, unroll=4)
+    lax.fori_loop(lo, hi, expand, 0, unroll=unroll)
 
 
 def advance(row, before, after, coef, c):
@@ -318,90 +335,151 @@
 
 NEAR = STEPS + 1
 FIN = 16 - STEPS
-
-
-def main(own, halo, msg_a, cor_a, table, ens, clim, near, kept, fin, first, second, ground, dense, coef):
-    odd = is_odd()
-    places = layout()
-
-    def take(r, _):
-        join(first, r + STEPS, halo[r], lambda q: own[r, q], places)
-        return 0
-
-    lax.fori_loop(0, ROWS, take, 0, unroll=16)
-    for k in range(STEPS):
-        join(first, STEPS - 1 - k, cor_a[k], [msg_a[k, g] for g in range(GROUPS)], places)
-    end = STEPS + ROWS
-
-    weigh(first, end, ground, dense, coef)
-    for n in range(NEAR):
-        near[n] = first[end - NEAR + n]
-
-    for s in range(STEPS):
-        src, dst = (first, second) if s % 2 == 0 else (second, first)
-        if s:
-            kept[s - 1, 0] = src[end - s - 2]
-            kept[s - 1, 1] = src[end - s - 1]
-
-        def step(r, _, src=src, dst=dst):
+CHUNK = 8
+
+
+EARLY = 4
+
+
+def walk(src, dst, coef, s):
+    lo, hi = STEPS + s + 1, STEPS + ROWS - s - 1
+
+    def step(n, _):
+        for e in range(CHUNK):
+            r = jnp.minimum(lo + n * CHUNK, hi - CHUNK) + e
             out = advance(lambda q: src[r, q], lambda q: src[r - 1, q], lambda q: src[r + 1, q], coef, r)
             for q in range(VECS):
                 dst[r, q] = out[q]
-            return 0
-
-        lax.fori_loop(s + 1, end - s - 1, step, 0, unroll=8)
+        return 0
+
+    lax.fori_loop(0, -(-(hi - lo) // CHUNK), step, 0)
+
+
+def keep(kept, n, state, s):
+    for d in range(2):
+        kept[0, n, d] = state[STEPS + s + 1 - d]
+        kept[1, n, d] = state[STEPS + ROWS - s - 2 + d]
+
+
+def start(own, got_1, got_2, table, state, coef, near, kept, second, edge, ground, dense):
+    west_first = west_is_first()
+    low = lanes() < HALF
+
+    def unpack(r, _):
+        a, b = got_1[r], got_2[r]
+        w, e = jnp.where(west_first, a, b), jnp.where(west_first, b, a)
+        edge[r] = jnp.where(low, w, pltpu.roll(e, HALF, 1))
+        edge[r + ROWS // 2] = jnp.where(low, pltpu.roll(w, HALF, 1), e)
+        return 0
+
+    lax.fori_loop(0, ROWS // 2, unpack, 0, unroll=8)
+
+    def take(m, _):
+        x = edge[pl.ds(m * 16, 16)].reshape(16 * 8, LANES)
+        parts = []
+        for _ in range(3):
+            parts.append(x.astype(BF16))
+            x = x - parts[-1].astype(F32)
+        lhs = jnp.concatenate(parts, axis=1)
+        for t in range(SETS):
+            out = dot(lhs, jnp.concatenate([table[t]] * 3, axis=0)).reshape(16, 8, PHASES * LANES)
+            for p in range(PHASES):
+                q = PHASES * t + p
+                rows = pl.ds(m * 16, 16)
+                state[pl.ds(STEPS + m * 16, 16), q] = own[rows, q] + out[:, :, LANES * p : LANES * p + LANES]
+        return 0
+
+    lax.fori_loop(0, ROWS // 16, take, 0, unroll=4)
+    end = STEPS + ROWS
+    weigh(state, end, STEPS + 1, end - 1, ground, dense, coef, 8)
+    for n in range(NEAR):
+        near[0, n] = state[2 * STEPS - n]
+        near[1, n] = state[end - NEAR + n]
+    for s in range(EARLY):
+        src, dst = (state, second) if s % 2 == 0 else (second, state)
+        walk(src, dst, coef, s)
+        keep(kept, s, dst, s + 1)
+
+
+def main(state, coef, table, ens, clim, kept, fin, first, second):
+    odd = is_odd()
+    src = state
+    for s in range(EARLY, STEPS):
+        dst = first if s % 2 else second
+        walk(src, dst, coef, s)
+        if s < STEPS - 1:
+            keep(kept, s - EARLY, dst, s + 1)
+        src = dst
+    end = STEPS + ROWS
     for n in range(FIN):
-        fin[n] = first[end - 16 + n]
+        fin[0, n] = first[STEPS + 15 - n]
+        fin[1, n] = first[end - 16 + n]
 
     def tile(m, _):
-        src = jnp.where(odd, m, ROWS // 16 - 1 - m)
-
         def row(n, q):
-            r = src * 16 + n
+            r = 16 * m + 16 + n
             return first[STEPS + jnp.where(odd, r, ROWS - 1 - r), q]
 
-        finish(row, odd, table, ens, clim, row_tile(src))
+        finish(row, odd, table, ens, clim, row_tile(m))
         return 0
 
-    lax.fori_loop(0, ROWS // 16 - 1, tile, 0)
-
-
-def tail(near, kept, fin, msg_b, cor_b, table, ens_in, clim_in, ens, clim, one, two, ground, dense, coef, ens_rows, clim_rows, sem):
-    del ens_in, clim_in
+    lax.fori_loop(0, ROWS // 16 - 2, tile, 0)
+
+
+def tail(
+    near, kept_a, kept_b, fin, msg_a, msg_b, rim_1, rim_2, table, ens_main, clim_main, ens, clim,
+    one, two, ground, dense, coef, ens_rows, clim_rows, sem,
+):
     odd = is_odd()
+    done = pl.ds(16, ROWS - 32)
+    copies = [
+        pltpu.make_async_copy(ens_main, ens.at[:, done, :], sem.at[0]),
+        pltpu.make_async_copy(clim_main, clim.at[:, done, :], sem.at[1]),
+    ]
+    for copy in copies:
+        copy.start()
     fold = lax.axis_index("lat") == lax.axis_size("lat") - 1
-    places = layout(fold)
-    for n in range(NEAR):
-        one[n] = near[n]
-    for k in range(STEPS):
-        join(one, NEAR + k, cor_b[k], [msg_b[k, g] for g in range(GROUPS)], places)
-    weigh(one, NEAR + STEPS, ground, dense, coef)
+    west_first = west_is_first()
+    low = lanes() < HALF
+    places = [layout(), layout(fold)]
+    for side, msg in enumerate((msg_a, msg_b)):
+        for n in range(NEAR):
+            one[16 * side + n] = near[side, n]
+        for k in range(STEPS):
+            cor = jnp.where(low == west_first, rim_1[side, k], rim_2[side, k])
+            join(one, 16 * side + NEAR + k, cor, [msg[k, g] for g in range(GROUPS)], places[side])
+    weigh(one, 32, 1, 31, ground, dense, coef, 10)
     for s in range(STEPS):
         src, dst = (one, two) if s % 2 == 0 else (two, one)
         lo = NEAR - 1 - s
-        if s:
-            src[lo - 1] = kept[s - 1, 0]
-            src[lo] = kept[s - 1, 1]
-        for n in range(lo, lo + STEPS):
-            out = advance(lambda q: src[n, q], lambda q: src[n - 1, q], lambda q: src[n + 1, q], coef, n)
-            for q in range(VECS):
-                dst[n, q] = out[q]
-    for n in range(FIN):
-        two[n] = fin[n]
-    for n in range(STEPS):
-        two[FIN + n] = one[1 + n]
-
-    def row(n, q):
-        return two[jnp.where(odd, n, 15 - n), q]
-
-    finish(row, odd, table, ens_rows, clim_rows, pl.ds(0, 16))
-    rows = row_tile(jnp.where(odd, ROWS // 16 - 1, 0))
-    copies = [
-        pltpu.make_async_copy(ens_rows, ens.at[:, rows, :], sem.at[0]),
-        pltpu.make_async_copy(clim_rows, clim.at[:, rows, :], sem.at[1]),
-    ]
-    for copy in copies:
-        copy.start()
+        kept, n = (kept_a, s - 1) if s <= EARLY else (kept_b, s - 1 - EARLY)
+        for side in range(2):
+            if s:
+                src[16 * side + lo - 1] = kept[side, n, 0]
+                src[16 * side + lo] = kept[side, n, 1]
+        for side in range(2):
+            for r in range(16 * side + lo, 16 * side + lo + STEPS):
+                out = advance(lambda q: src[r, q], lambda q: src[r - 1, q], lambda q: src[r + 1, q], coef, r)
+                for q in range(VECS):
+                    dst[r, q] = out[q]
+    for side in range(2):
+        for n in range(FIN):
+            two[16 * side + n] = fin[side, n]
+        for n in range(STEPS):
+            two[16 * side + FIN + n] = one[16 * side + 1 + n]
+        rising = odd if side else ~odd
+
+        def row(n, q):
+            return two[16 * side + jnp.where(rising, n, 15 - n), q]
+
+        finish(row, odd, table, ens_rows.at[side], clim_rows.at[side], pl.ds(0, 16))
+        rows = row_tile(jnp.where(rising, ROWS // 16 - 1, 0))
+        copies += [
+            pltpu.make_async_copy(ens_rows.at[side], ens.at[:, rows, :], sem.at[2 + 2 * side]),
+            pltpu.make_async_copy(clim_rows.at[side], clim.at[:, rows, :], sem.at[3 + 2 * side]),
+        ]
+        for copy in copies[-2:]:
+            copy.start()
     for copy in copies:
         copy.wait()
 
@@ -423,62 +501,69 @@
     route_b = route(pair_b)
     route_1 = route(lambda i, l: (i ^ 1, l))
     route_2 = route(lambda i, l: ((i + (1 if i % 2 else -1)) % n_lon, l))
-    table_edge, table_in = tables()
+    table_edge, table_in, table_halo = tables()
     count = members.shape[0] * 2
     arrays = (members.reshape(count, ROWS, LANES), increment, climate_spread, diffusivity, inverse_area, land_sea)
     side = (STEPS, GROUPS, *TILE)
-    hbm = [pl.BlockSpec(memory_space=pltpu.HBM)] * 8
+    hbm = [pl.BlockSpec(memory_space=pltpu.HBM)] * 9
     two = (2, ROWS, LANES)
-    msg_a, msg_b, msg_e, mem_v, src_v, into_v = call(
+    packed = ((ROWS // 2, *TILE), F32)
+    msg_a, msg_b, msg_1, msg_2, mem_v, src_v, into_v, tab_h_v = call(
         edges,
         "edges",
-        [(side, F32), (side, F32), ((ROWS, *TILE), F32)]
-        + [((count, ROWS, LANES), BF16), ((6, ROWS, LANES), F32), (table_in.shape, BF16)],
-        8,
-        [pltpu.VMEM((2, *side), F32), pltpu.VMEM(two, F32), pltpu.VMEM(two, F32)]
+        [(side, F32), (side, F32), packed, packed]
+        + [((count, ROWS, LANES), BF16), ((6, ROWS, LANES), F32), (table_in.shape, BF16), (table_halo.shape, BF16)],
+        9,
+        [pltpu.VMEM((2, *side), F32), pltpu.VMEM((ROWS, *TILE), F32), pltpu.VMEM(two, F32), pltpu.VMEM(two, F32)]
         + [pltpu.VMEM((ROWS, LANES), d) for d in (F32, F32, jnp.int32)]
-        + [pltpu.VMEM(table_edge.shape, BF16), pltpu.SemaphoreType.DMA((11,))],
+        + [pltpu.VMEM(table_edge.shape, BF16), pltpu.SemaphoreType.DMA((12,))],
         limit=12,
         in_specs=hbm,
-    )(*[pltpu.with_memory_space_constraint(x, pltpu.HBM) for x in (*arrays, table_edge, table_in)])
+    )(*[pltpu.with_memory_space_constraint(x, pltpu.HBM) for x in (*arrays, table_edge, table_in, table_halo)])
     got_b = lax.ppermute(msg_b, AXES, route_b)
     got_a = lax.ppermute(msg_a, AXES, route_a)
-    p1 = lax.ppermute(msg_e, AXES, route_1)
-    p2 = lax.ppermute(msg_e, AXES, route_2)
+    got_2 = lax.ppermute(msg_2, AXES, route_2)
+    got_1 = lax.ppermute(msg_1, AXES, route_1)
     (own,) = call(spread, "spread", [((ROWS, VECS, *TILE), F32)], 3, limit=12)(mem_v, src_v, into_v)
-    p1, p2, own = lax.optimization_barrier((p1, p2, own))
-    halo, cor_a, cor_b = call(
-        corner, "corner", [((ROWS, *TILE), F32), ((STEPS, *TILE), F32), ((STEPS, *TILE), F32)], 2, limit=4
-    )(p1, p2)
-    cor_a = lax.ppermute(cor_a, AXES, route_a)
-    cor_b = lax.ppermute(cor_b, AXES, route_b)
+    got_1, got_2, own = lax.optimization_barrier((got_1, got_2, own))
+    vecs = (VECS, *TILE)
+    state, coef, near, kept_a = call(
+        start,
+        "start",
+        [((EXT, *vecs), F32), ((EXT, 5 * PHASES, *TILE), F32), ((2, NEAR, *vecs), F32), ((2, EARLY, 2, *vecs), F32)],
+        4,
+        [pltpu.VMEM((EXT, *vecs), F32), pltpu.VMEM((ROWS, *TILE), F32)]
+        + [pltpu.VMEM((n, EXT + 20, LANES), F32) for n in (2 * PHASES, 5 * PHASES)],
+        limit=20,
+        cost=(10**11, 10**8),
+    )(own, got_1, got_2, tab_h_v)
+    got_a, got_b, state = lax.optimization_barrier((got_a, got_b, state))
+    (rim,) = call(rim_of_halo, "rim", [((2, STEPS, *TILE), F32)], 2, limit=4)(got_a, got_b)
+    rim_1 = lax.ppermute(rim, AXES, route_1)
+    rim_2 = lax.ppermute(rim, AXES, route_2)
     full = [((count, ROWS, LANES), BF16), ((2, ROWS, LANES), F32)]
-    vecs = (VECS, *TILE)
-    ens, clim, near, kept, fin = call(
+    most = [((count, ROWS - 32, LANES), BF16), ((2, ROWS - 32, LANES), F32)]
+    ens, clim, kept_b, fin = call(
         main,
         "main",
-        full + [((NEAR, *vecs), F32), ((STEPS - 1, 2, *vecs), F32), ((FIN, *vecs), F32)],
-        5,
-        [pltpu.VMEM((EXT, *vecs), F32)] * 2
-        + [pltpu.VMEM((n, EXT + 20, LANES), F32) for n in (2 * PHASES, 5 * PHASES)]
-        + [pltpu.VMEM((EXT, 5 * PHASES, *TILE), F32)],
-        limit=32,
-    )(own, halo, got_a, cor_a, into_v)
-    anywhere = [pl.BlockSpec(memory_space=pl.ANY)] * 2
+        most + [((2, STEPS - EARLY - 1, 2, *vecs), F32), ((2, FIN, *vecs), F32)],
+        3,
+        [pltpu.VMEM((EXT, *vecs), F32)] * 2,
+        limit=20,
+        cost=(10**11, 10**8),
+    )(state, coef, into_v)
     ens, clim = call(
         tail,
         "tail",
         full,
-        8,
-        [pltpu.VMEM((16, *vecs), F32)] * 2
-        + [pltpu.VMEM((n, 32, LANES), F32) for n in (2 * PHASES, 5 * PHASES)]
-        + [pltpu.VMEM((16, 5 * PHASES, *TILE), F32)]
-        + [pltpu.VMEM((count, 16, LANES), BF16), pltpu.VMEM((2, 16, LANES), F32), pltpu.SemaphoreType.DMA((2,))],
-        limit=12,
-        in_specs=vmem(6) + anywhere,
-        out_specs=anywhere,
-        aliases={6: 0, 7: 1},
-    )(near, kept, fin, got_b, cor_b, into_v, ens, clim)
+        11,
+        [pltpu.VMEM((32, *vecs), F32)] * 2
+        + [pltpu.VMEM((n, 48, LANES), F32) for n in (2 * PHASES, 5 * PHASES)]
+        + [pltpu.VMEM((32, 5 * PHASES, *TILE), F32)]
+        + [pltpu.VMEM((2, count, 16, LANES), BF16), pltpu.VMEM((2, 2, 16, LANES), F32), pltpu.SemaphoreType.DMA((6,))],
+        limit=16,
+        out_specs=[pl.BlockSpec(memory_space=pltpu.HBM)] * 2,
+    )(near, kept_a, kept_b, fin, got_a, got_b, rim_1, rim_2, into_v, ens, clim)
     return ens.reshape(members.shape), clim
 
 

time: 39.2 us -> 35.5 us (0.906)
  starting transfers between devices: 18.1 us -> 13.8 us
  waiting for transfers between devices: 0.02 us -> 3 us
  Pallas kernels: 20.2 us -> 17.8 us
    ppermute x4, starting transfers between devices: 15.1 us -> 5.06 us  [the longest x1 3.3 us: body(): rim_1 = lax.ppermute(rim, AXES, route_1)]
    ppermute x1, starting transfers between devices: 2.61 us -> 8.31 us  [body(): got_b = lax.ppermute(msg_b, AXES, route_b)]
    ppermute x1, waiting for transfers between devices: 0.01 us -> 2.99 us  [body(): got_b = lax.ppermute(msg_b, AXES, route_b)]
    pallas_call x4 -> x5, Pallas kernels: 18.5 us -> 16.1 us  [the longest x1 6.09 us: body(): call(start, 'start', [((EXT, *vecs), F32), ((EXT, 5 * PHASES, *TILE), F32...]
  transfers between devices with their start and end apart: 6 -> 6, of which waited for: 0 -> 1; matrix products, arithmetic and copies ran while one was open for 0% -> 0% of each run, Pallas kernels for 39% -> 30%
where the time goes in v1:
time: 35.5 us; the launch traced here: 35.4 us
  Pallas kernels  17.8 us (50%)
  starting transfers between devices  13.8 us (39%)
  waiting for transfers between devices  3 us (8%)
  between operations  0.72 us (2%)
    ppermute x1, starting transfers between devices, body(): got_b = lax.ppermute(msg_b, AXES, route_b)  8.31 us
    pallas_call x1, Pallas kernels, body(): call(start, 'start', [((EXT, *vecs), F32), ((EXT, 5 * PHASES, *TILE), F32...  6.09 us
    pallas_call x1, Pallas kernels, body(): call(tail, 'tail', full, 11, [pltpu.VMEM((32, *vecs), F32)] * 2 + [pltpu....  4.8 us
    ppermute x1, starting transfers between devices, body(): rim_1 = lax.ppermute(rim, AXES, route_1)  3.3 us
    ppermute x1, waiting for transfers between devices, body(): got_b = lax.ppermute(msg_b, AXES, route_b)  2.99 us
    pallas_call x1, Pallas kernels, body(): call(main, 'main', most + [((2, STEPS - EARLY - 1, 2, *vecs), F32), ((2,...  2.82 us
    pallas_call x1, Pallas kernels, body(): call(edges, 'edges', [(side, F32), (side, F32), packed, packed] + [((coun...  2.17 us
    pallas_call x1, Pallas kernels, body(): call(spread, 'spread', [((ROWS, VECS, *TILE), F32)], 3, limit=12)  1.75 us
  transfers between devices with their start and end apart: 6, of which 1 were waited for; matrix products, arithmetic and copies ran while one was open for 0% of the time, Pallas kernels for 30%

profile of v1, /device:TPU:29, one launch (start us, length us, event | category | flops | bytes accessed | tf_op | source)
XLA Modules:
  0.0 35.4 jit_solution(5980856624725712837)
XLA Ops:
  0.6 2.2 %edges.1 = (f32[6,9,8,128]{3,2,1,0:T(8,128)S(1)}, f32[6,9,8,128]{3,2,1,0:T(8,128)S(1)}, f32[32,8,128]{2,1,0:T(8,128)S(1)}, f32[32,8,128]{2,1,0:T(8,128)S(1)}, bf...) custom-call(bf16[64,64,128]{2,1,0:T(8,128)(2,1)} %bitcast.2, ...), custom_call_target="tpu_custom_call" | custom-call | tf_op jit(solution)/shard_map/edges/pallas_call | solution.py:511
  2.8 0.8 %collective-permute-start = (f32[32,8,128]{2,1,0:T(8,128)S(1)}, f32[32,8,128]{2,1,0:T(8,128)S(1)}, u32[]{:S(2)}, u32[]{:S(2)}) collective-permute-start(f32[32,8,128]{2,1,0:T(8,128)S(1)} %get-tuple-element.26), channel_id=1, source_target_pairs={{0,8},{1,9},{2,10},{3,11},{4,12},{5,13},{6,14},{7,15},{8,0},{9,1},... | collective-permute-start | bytes 393224 | tf_op jit(solution)/shard_map/ppermute | solution.py:526
  3.6 0.9 %collective-permute-start.1 = (f32[32,8,128]{2,1,0:T(8,128)S(1)}, f32[32,8,128]{2,1,0:T(8,128)S(1)}, u32[]{:S(2)}, u32[]{:S(2)}) collective-permute-start(f32[32,8,128]{2,1,0:T(8,128)S(1)} %get-tuple-element.27), channel_id=1, source_target_pairs={{0,248},{1,249},{2,250},{3,251},{4,252},{5,253},{6,254},{7,255},{8... | collective-permute-start | bytes 393224 | tf_op jit(solution)/shard_map/ppermute | solution.py:525
  4.5 0.5 %collective-permute-start.2 = (f32[6,9,8,128]{3,2,1,0:T(8,128)S(1)}, f32[6,9,8,128]{3,2,1,0:T(8,128)S(1)}, u32[]{:S(2)}, u32[]{:S(2)}) collective-permute-start(f32[6,9,8,128]{3,2,1,0:T(8,128)S(1)} %get-tuple-element.37), channel_id=1, source_target_pairs={{0,1},{1,0},{2,3},{3,2},{4,5},{5,4},{6,7},{7,6},{8,9},{9,8},{10,11... | collective-permute-start | bytes 663560 | tf_op jit(solution)/shard_map/ppermute | solution.py:524
  4.9 8.3 %collective-permute-start.3 = (f32[6,9,8,128]{3,2,1,0:T(8,128)S(1)}, f32[6,9,8,128]{3,2,1,0:T(8,128)S(1)}, u32[]{:S(2)}, u32[]{:S(2)}) collective-permute-start(f32[6,9,8,128]{3,2,1,0:T(8,128)S(1)} %get-tuple-element.38), channel_id=1, source_target_pairs={{1,2},{2,1},{3,4},{4,3},{5,6},{6,5},{7,255},{9,10},{10,9},{11,12},... | collective-permute-start | bytes 663560 | tf_op jit(solution)/shard_map/ppermute | solution.py:523
  13.3 1.8 %spread.1.own = f32[64,12,8,128]{3,2,1,0:T(8,128)S(1)} custom-call(bf16[64,64,128]{2,1,0:T(8,128)(2,1)S(1)} %get-tuple-element.28.mem, f32[6,64,128]{2,1,0:T(8,128)S(1)} %get-tuple-element.29.src, bf16[384,512]{1,0:T(8,128)(2,1)S(1)} %get-tuple-element.30.table), custom_call_target="tpu_custom_call" | custom-call | tf_op jit(solution)/shard_map/spread/pallas_call | solution.py:527
  15.0 0.0 collective-permute-done.got_1
  15.0 0.0 collective-permute-done.1.got_2
  15.0 6.1 %start.1 = (f32[76,12,8,128]{3,2,1,0:T(8,128)S(1)}, f32[76,20,8,128]{3,2,1,0:T(8,128)S(1)}, f32[2,7,12,8,128]{4,3,2,1,0:T(8,128)S(1)}, f32[2,4,2,12,8,128]{5,4,3,2,1,0:T(8,128)S(1)}) custom-call(f32[64,12,8,128]{3,2,1,0:T(8,128)S(1)} %spread.1.own, f32[32,8,128]{2,1,0:T(8,128)S(1)} %collective-permute-done.got_1, ...), custom_call_target="tpu_custom_call" | custom-call | flops 99999997952 | bytes 100000000 | tf_op jit(solution)/shard_map/start/pallas_call | solution.py:530
  21.1 0.0 collective-permute-done.2.msg_a
  21.2 3.0 %collective-permute-done.3.msg_b = f32[6,9,8,128]{3,2,1,0:T(8,128)S(1)} collective-permute-done((f32[6,9,8,128]{3,2,1,0:T(8,128)S(1)}, f32[6,9,8,128]{3,2,1,0:T(8,128)S(1)}, u32[]{:S(2)}, u32[]{:S(2)}) %collective-permute-start.3) | collective-permute-done | bytes 221216 | tf_op jit(solution)/shard_map/ppermute | solution.py:523
  24.1 0.2 rim.1
  24.3 0.1 collective-permute-start.5
  24.4 3.3 %collective-permute-start.4 = (f32[2,6,8,128]{3,2,1,0:T(8,128)S(1)}, f32[2,6,8,128]{3,2,1,0:T(8,128)S(1)}, u32[]{:S(2)}, u32[]{:S(2)}) collective-permute-start(f32[2,6,8,128]{3,2,1,0:T(8,128)S(1)} %rim.1), channel_id=1, source_target_pairs={{0,8},{1,9},{2,10},{3,11},{4,12},{5,13},{6,14},{7,15},{8,0},{9,1},... | collective-permute-start | bytes 147464 | tf_op jit(solution)/shard_map/ppermute | solution.py:542
  27.7 2.8 %main.1 = (bf16[64,32,128]{2,1,0:T(8,128)(2,1)S(1)}, f32[2,32,128]{2,1,0:T(8,128)S(1)}, f32[2,1,2,12,8,128]{5,4,3,2,1,0:T(8,128)S(1)}, f32[2,10,12,8,128]{4,3,2,1,0:T(8,128)S(1)}) custom-call(f32[76,12,8,128]{3,2,1,0:T(8,128)S(1)} %get-tuple-element.40.state, f32[76,20,8,128]{3,2,1,0:T(8,128)S(1)} %get-tuple-element.41.coef, ...), custom_call_target="tpu_custom_call" | custom-call | flops 99999997952 | bytes 100000000 | tf_op jit(solution)/shard_map/main/pallas_call | solution.py:546
  30.6 0.0 collective-permute-done.5.rim_2
  30.6 0.0 collective-permute-done.4.rim_1
  30.6 4.8 %tail.1 = (bf16[64,64,128]{2,1,0:T(8,128)(2,1)}, f32[2,64,128]{2,1,0:T(8,128)}) custom-call(f32[2,7,12,8,128]{4,3,2,1,0:T(8,128)S(1)} %get-tuple-element.35.near, f32[2,4,2,12,8,128]{5,4,3,2,1,0:T(8,128)S(1)} %get-tuple-element.36.kept_a, f32[2,1,2,12,8,128]{5,4,3,2,1,0:T(8,128)S(1)} %get-tuple-element.42.kept_b, ...), custom_call_target="tpu_custom_call" | custom-call | tf_op jit(solution)/shard_map/tail/pallas_call | solution.py:555
Async XLA Ops:
  2.8 12.2 %collective-permute-start = (f32[32,8,128]{2,1,0:T(8,128)S(1)}, f32[32,8,128]{2,1,0:T(8,128)S(1)}, u32[]{:S(2)}, u32[]{:S(2)}) collective-permute-start(f32[32,8,128]{2,1,0:T(8,128)S(1)} %get-tuple-element.26), channel_id=1, source_target_pairs={{0,8},{1,9},{2,10},{3,11},{4,12},{5,13},{6,14},{7,15},{8,0},{9,1},... | collective-permute-start | bytes 393224 | tf_op jit(solution)/shard_map/ppermute | solution.py:526
  3.6 11.5 %collective-permute-start.1 = (f32[32,8,128]{2,1,0:T(8,128)S(1)}, f32[32,8,128]{2,1,0:T(8,128)S(1)}, u32[]{:S(2)}, u32[]{:S(2)}) collective-permute-start(f32[32,8,128]{2,1,0:T(8,128)S(1)} %get-tuple-element.27), channel_id=1, source_target_pairs={{0,248},{1,249},{2,250},{3,251},{4,252},{5,253},{6,254},{7,255},{8... | collective-permute-start | bytes 393224 | tf_op jit(solution)/shard_map/ppermute | solution.py:525
  4.5 16.7 %collective-permute-start.2 = (f32[6,9,8,128]{3,2,1,0:T(8,128)S(1)}, f32[6,9,8,128]{3,2,1,0:T(8,128)S(1)}, u32[]{:S(2)}, u32[]{:S(2)}) collective-permute-start(f32[6,9,8,128]{3,2,1,0:T(8,128)S(1)} %get-tuple-element.37), channel_id=1, source_target_pairs={{0,1},{1,0},{2,3},{3,2},{4,5},{5,4},{6,7},{7,6},{8,9},{9,8},{10,11... | collective-permute-start | bytes 663560 | tf_op jit(solution)/shard_map/ppermute | solution.py:524
  4.9 19.2 %collective-permute-start.3 = (f32[6,9,8,128]{3,2,1,0:T(8,128)S(1)}, f32[6,9,8,128]{3,2,1,0:T(8,128)S(1)}, u32[]{:S(2)}, u32[]{:S(2)}) collective-permute-start(f32[6,9,8,128]{3,2,1,0:T(8,128)S(1)} %get-tuple-element.38), channel_id=1, source_target_pairs={{1,2},{2,1},{3,4},{4,3},{5,6},{6,5},{7,255},{9,10},{10,9},{11,12},... | collective-permute-start | bytes 663560 | tf_op jit(solution)/shard_map/ppermute | solution.py:523
  24.3 6.2 %collective-permute-start.5 = (f32[2,6,8,128]{3,2,1,0:T(8,128)S(1)}, f32[2,6,8,128]{3,2,1,0:T(8,128)S(1)}, u32[]{:S(2)}, u32[]{:S(2)}) collective-permute-start(f32[2,6,8,128]{3,2,1,0:T(8,128)S(1)} %rim.1), channel_id=1, source_target_pairs={{0,248},{1,249},{2,250},{3,251},{4,252},{5,253},{6,254},{7,255},{8... | collective-permute-start | bytes 147464 | tf_op jit(solution)/shard_map/ppermute | solution.py:543
  24.4 6.1 %collective-permute-start.4 = (f32[2,6,8,128]{3,2,1,0:T(8,128)S(1)}, f32[2,6,8,128]{3,2,1,0:T(8,128)S(1)}, u32[]{:S(2)}, u32[]{:S(2)}) collective-permute-start(f32[2,6,8,128]{3,2,1,0:T(8,128)S(1)} %rim.1), channel_id=1, source_target_pairs={{0,8},{1,9},{2,10},{3,11},{4,12},{5,13},{6,14},{7,15},{8,0},{9,1},... | collective-permute-start | bytes 147464 | tf_op jit(solution)/shard_map/ppermute | solution.py:542

commit v2 on v1

--- a/solution.py
+++ b/solution.py
@@ -21,6 +21,7 @@
 HALF = LANES // 2
 EXT = ROWS + 2 * STEPS
 TILE = (8, LANES)
+NEAR = STEPS + 1
 AXES = ("lon", "lat")
 F32 = jnp.float32
 BF16 = jnp.bfloat16
@@ -71,7 +72,7 @@
     return [pl.BlockSpec(memory_space=pltpu.VMEM)] * n
 
 
-def call(kernel, name, outs, n_in, scratch=(), limit=16, cost=(0, 0), in_specs=None, out_specs=None):
+def call(kernel, name, outs, n_in, scratch=(), limit=16, cost=(0, 0), in_specs=None, out_specs=None, aliases=None):
     return pl.pallas_call(
         kernel,
         name=name,
@@ -79,13 +80,14 @@
         in_specs=in_specs or vmem(n_in),
         out_specs=out_specs or vmem(len(outs)),
         scratch_shapes=list(scratch),
+        input_output_aliases=aliases or {},
         compiler_params=pltpu.CompilerParams(vmem_limit_bytes=limit * MIB),
         cost_estimate=pl.CostEstimate(flops=cost[0], bytes_accessed=cost[1], transcendentals=0),
     )
 
 
 def edges(
-    mem, inc, clim, dif, inv, land, table, into, tab_h, msg_a, msg_b, msg_1, msg_2, mem_v, src_v, into_v, tab_h_v,
+    mem, inc, clim, dif, inv, land, table, into, tab_h, msg_a, msg_b, msg_1, msg_2, mem_v, src_v, into_v, tab_h_v, own,
     side_rows, rim, inc_v, clim_v, dif_v, inv_v, land_v, table_v, sem,
 ):
     pairs = [(inc, inc_v), (land, land_v), (clim, clim_v), (dif, dif_v), (inv, inv_v)]
@@ -156,6 +158,10 @@
     for copy in copies[10:]:
         copy.wait()
 
+    @pl.when(first_out())
+    def _():
+        deal(mem_v, src_v, into_v, own)
+
 
 def rim_column():
     lane = lanes()
@@ -177,7 +183,19 @@
     return out
 
 
-def spread(mem, src, table, state):
+def first_out():
+    return lax.axis_index("lon") < 4
+
+
+def spread(mem, src, table, before, state):
+    del before
+
+    @pl.when(~first_out())
+    def _():
+        deal(mem, src, table, state)
+
+
+def deal(mem, src, table, state):
     odd = is_odd()
     part = lanes() // SPAN
     places = layout()
@@ -225,16 +243,25 @@
     return lax.rem(lax.axis_index("lon"), 2) == 1
 
 
-def join(state, r, cor, main, places):
+def layouts():
+    return [layout(), layout(lax.axis_index("lat") == lax.axis_size("lat") - 1)]
+
+
+def near_rows(near, msg_a, msg_b, rows):
     part = lanes() // SPAN
-    for t in range(SETS):
-        for p in range(PHASES):
-            column, is_halo, place = places[p]
-            x = gather(cor, place + SETS * STEPS * t)
-            own = gather(main[3 * t], column)
-            for k in (1, 2):
-                own = jnp.where(part == k, gather(main[3 * t + k], column), own)
-            state[r, PHASES * t + p] = jnp.where(is_halo, x, own)
+    places = layouts()
+    for side, msg in enumerate((msg_a, msg_b)):
+        for n in range(NEAR):
+            rows[16 * side + n] = near[side, n]
+        for k in range(STEPS):
+            x = [msg[k, g] for g in range(GROUPS)]
+            for t in range(SETS):
+                for p in range(PHASES):
+                    column = places[side][p][0]
+                    own = gather(x[3 * t], column)
+                    for n in (1, 2):
+                        own = jnp.where(part == n, gather(x[3 * t + n], column), own)
+                    rows[16 * side + NEAR + k, PHASES * t + p] = own
 
 
 def flat(ref):
@@ -333,12 +360,8 @@
             ens_out[pl.ds(8 * (3 * t + k), 8), rows, :] = out[:, LANES * k : LANES * k + LANES].reshape(8, 16, LANES)
 
 
-NEAR = STEPS + 1
 FIN = 16 - STEPS
 CHUNK = 8
-
-
-EARLY = 4
 
 
 def walk(src, dst, coef, s):
@@ -361,7 +384,7 @@
         kept[1, n, d] = state[STEPS + ROWS - s - 2 + d]
 
 
-def start(own, got_1, got_2, table, state, coef, near, kept, second, edge, ground, dense):
+def start(own, got_1, got_2, table, state, near, kept, fin, coef, second, edge, ground, dense):
     west_first = west_is_first()
     low = lanes() < HALF
 
@@ -395,30 +418,23 @@
     for n in range(NEAR):
         near[0, n] = state[2 * STEPS - n]
         near[1, n] = state[end - NEAR + n]
-    for s in range(EARLY):
+    for s in range(STEPS):
         src, dst = (state, second) if s % 2 == 0 else (second, state)
         walk(src, dst, coef, s)
-        keep(kept, s, dst, s + 1)
-
-
-def main(state, coef, table, ens, clim, kept, fin, first, second):
+        if s < STEPS - 1:
+            keep(kept, s, dst, s + 1)
+    for n in range(FIN):
+        fin[0, n] = state[STEPS + 15 - n]
+        fin[1, n] = state[end - 16 + n]
+
+
+def main(state, table, ens, clim):
     odd = is_odd()
-    src = state
-    for s in range(EARLY, STEPS):
-        dst = first if s % 2 else second
-        walk(src, dst, coef, s)
-        if s < STEPS - 1:
-            keep(kept, s - EARLY, dst, s + 1)
-        src = dst
-    end = STEPS + ROWS
-    for n in range(FIN):
-        fin[0, n] = first[STEPS + 15 - n]
-        fin[1, n] = first[end - 16 + n]
 
     def tile(m, _):
         def row(n, q):
             r = 16 * m + 16 + n
-            return first[STEPS + jnp.where(odd, r, ROWS - 1 - r), q]
+            return state[STEPS + jnp.where(odd, r, ROWS - 1 - r), q]
 
         finish(row, odd, table, ens, clim, row_tile(m))
         return 0
@@ -427,7 +443,7 @@
 
 
 def tail(
-    near, kept_a, kept_b, fin, msg_a, msg_b, rim_1, rim_2, table, ens_main, clim_main, ens, clim,
+    rows_in, kept, fin, rim_1, rim_2, table, ens_main, clim_main, ens, clim,
     one, two, ground, dense, coef, ens_rows, clim_rows, sem,
 ):
     odd = is_odd()
@@ -438,25 +454,28 @@
     ]
     for copy in copies:
         copy.start()
-    fold = lax.axis_index("lat") == lax.axis_size("lat") - 1
     west_first = west_is_first()
     low = lanes() < HALF
-    places = [layout(), layout(fold)]
-    for side, msg in enumerate((msg_a, msg_b)):
+    places = layout()
+    for side in range(2):
         for n in range(NEAR):
-            one[16 * side + n] = near[side, n]
+            one[16 * side + n] = rows_in[16 * side + n]
         for k in range(STEPS):
+            r = 16 * side + NEAR + k
             cor = jnp.where(low == west_first, rim_1[side, k], rim_2[side, k])
-            join(one, 16 * side + NEAR + k, cor, [msg[k, g] for g in range(GROUPS)], places[side])
+            for t in range(SETS):
+                for p in range(PHASES):
+                    _, is_halo, place = places[p]
+                    x = gather(cor, place + SETS * STEPS * t)
+                    one[r, PHASES * t + p] = jnp.where(is_halo, x, rows_in[r, PHASES * t + p])
     weigh(one, 32, 1, 31, ground, dense, coef, 10)
     for s in range(STEPS):
         src, dst = (one, two) if s % 2 == 0 else (two, one)
         lo = NEAR - 1 - s
-        kept, n = (kept_a, s - 1) if s <= EARLY else (kept_b, s - 1 - EARLY)
         for side in range(2):
             if s:
-                src[16 * side + lo - 1] = kept[side, n, 0]
-                src[16 * side + lo] = kept[side, n, 1]
+                src[16 * side + lo - 1] = kept[side, s - 1, 0]
+                src[16 * side + lo] = kept[side, s - 1, 1]
         for side in range(2):
             for r in range(16 * side + lo, 16 * side + lo + STEPS):
                 out = advance(lambda q: src[r, q], lambda q: src[r - 1, q], lambda q: src[r + 1, q], coef, r)
@@ -508,33 +527,36 @@
     hbm = [pl.BlockSpec(memory_space=pltpu.HBM)] * 9
     two = (2, ROWS, LANES)
     packed = ((ROWS // 2, *TILE), F32)
-    msg_a, msg_b, msg_1, msg_2, mem_v, src_v, into_v, tab_h_v = call(
+    msg_a, msg_b, msg_1, msg_2, mem_v, src_v, into_v, tab_h_v, own = call(
         edges,
         "edges",
         [(side, F32), (side, F32), packed, packed]
-        + [((count, ROWS, LANES), BF16), ((6, ROWS, LANES), F32), (table_in.shape, BF16), (table_halo.shape, BF16)],
+        + [((count, ROWS, LANES), BF16), ((6, ROWS, LANES), F32), (table_in.shape, BF16), (table_halo.shape, BF16)]
+        + [((ROWS, VECS, *TILE), F32)],
         9,
         [pltpu.VMEM((2, *side), F32), pltpu.VMEM((ROWS, *TILE), F32), pltpu.VMEM(two, F32), pltpu.VMEM(two, F32)]
         + [pltpu.VMEM((ROWS, LANES), d) for d in (F32, F32, jnp.int32)]
         + [pltpu.VMEM(table_edge.shape, BF16), pltpu.SemaphoreType.DMA((12,))],
-        limit=12,
+        limit=6,
         in_specs=hbm,
     )(*[pltpu.with_memory_space_constraint(x, pltpu.HBM) for x in (*arrays, table_edge, table_in, table_halo)])
     got_b = lax.ppermute(msg_b, AXES, route_b)
     got_a = lax.ppermute(msg_a, AXES, route_a)
     got_2 = lax.ppermute(msg_2, AXES, route_2)
     got_1 = lax.ppermute(msg_1, AXES, route_1)
-    (own,) = call(spread, "spread", [((ROWS, VECS, *TILE), F32)], 3, limit=12)(mem_v, src_v, into_v)
+    (own,) = call(spread, "spread", [((ROWS, VECS, *TILE), F32)], 4, limit=5, aliases={3: 0})(
+        mem_v, src_v, into_v, own
+    )
     got_1, got_2, own = lax.optimization_barrier((got_1, got_2, own))
     vecs = (VECS, *TILE)
-    state, coef, near, kept_a = call(
+    state, near, kept, fin = call(
         start,
         "start",
-        [((EXT, *vecs), F32), ((EXT, 5 * PHASES, *TILE), F32), ((2, NEAR, *vecs), F32), ((2, EARLY, 2, *vecs), F32)],
+        [((EXT, *vecs), F32), ((2, NEAR, *vecs), F32), ((2, STEPS - 1, 2, *vecs), F32), ((2, FIN, *vecs), F32)],
         4,
-        [pltpu.VMEM((EXT, *vecs), F32), pltpu.VMEM((ROWS, *TILE), F32)]
+        [pltpu.VMEM((EXT, 5 * PHASES, *TILE), F32), pltpu.VMEM((EXT, *vecs), F32), pltpu.VMEM((ROWS, *TILE), F32)]
         + [pltpu.VMEM((n, EXT + 20, LANES), F32) for n in (2 * PHASES, 5 * PHASES)],
-        limit=20,
+        limit=14,
         cost=(10**11, 10**8),
     )(own, got_1, got_2, tab_h_v)
     got_a, got_b, state = lax.optimization_barrier((got_a, got_b, state))
@@ -543,27 +565,21 @@
     rim_2 = lax.ppermute(rim, AXES, route_2)
     full = [((count, ROWS, LANES), BF16), ((2, ROWS, LANES), F32)]
     most = [((count, ROWS - 32, LANES), BF16), ((2, ROWS - 32, LANES), F32)]
-    ens, clim, kept_b, fin = call(
-        main,
-        "main",
-        most + [((2, STEPS - EARLY - 1, 2, *vecs), F32), ((2, FIN, *vecs), F32)],
-        3,
-        [pltpu.VMEM((EXT, *vecs), F32)] * 2,
-        limit=20,
-        cost=(10**11, 10**8),
-    )(state, coef, into_v)
+    rim, near = lax.optimization_barrier((rim, near))
+    (rows,) = call(near_rows, "near_rows", [((32, *vecs), F32)], 3, limit=4)(near, got_a, got_b)
+    ens, clim = call(main, "main", most, 2, limit=5)(state, into_v)
     ens, clim = call(
         tail,
         "tail",
         full,
-        11,
+        8,
         [pltpu.VMEM((32, *vecs), F32)] * 2
         + [pltpu.VMEM((n, 48, LANES), F32) for n in (2 * PHASES, 5 * PHASES)]
         + [pltpu.VMEM((32, 5 * PHASES, *TILE), F32)]
         + [pltpu.VMEM((2, count, 16, LANES), BF16), pltpu.VMEM((2, 2, 16, LANES), F32), pltpu.SemaphoreType.DMA((6,))],
-        limit=16,
+        limit=8,
         out_specs=[pl.BlockSpec(memory_space=pltpu.HBM)] * 2,
-    )(near, kept_a, kept_b, fin, got_a, got_b, rim_1, rim_2, into_v, ens, clim)
+    )(rows, kept, fin, rim_1, rim_2, into_v, ens, clim)
     return ens.reshape(members.shape), clim
 
 

time: 35.5 us -> 33.9 us (0.955)
  starting transfers between devices: 13.8 us -> 12.6 us
  waiting for transfers between devices: 3 us -> 2.38 us
    ppermute x1, starting transfers between devices: 8.31 us -> 6.55 us  [body(): got_b = lax.ppermute(msg_b, AXES, route_b)]
    pallas_call x1, Pallas kernels: 2.17 us -> 3.93 us  [body(): call(edges, 'edges', [(side, F32), (side, F32), packed, packed] + [((coun...]
    pallas_call x4 -> x5, Pallas kernels: 15.5 us -> 13.8 us  [the longest x1 7.96 us: body(): call(start, 'start', [((EXT, *vecs), F32), ((2, NEAR, *vecs), F32), ((2,...]
    ppermute x1, waiting for transfers between devices: 2.99 us -> 2.37 us  [body(): got_b = lax.ppermute(msg_b, AXES, route_b)]
    ppermute x1, starting transfers between devices: 0.09 us -> 0.49 us  [body(): rim_2 = lax.ppermute(rim, AXES, route_2)]
where the time goes in v2:
time: 33.9 us; the launch traced here: 33.6 us
  Pallas kernels  17.9 us (53%)
  starting transfers between devices  12.6 us (37%)
  waiting for transfers between devices  2.38 us (7%)
  between operations  0.71 us (2%)
    pallas_call x1, Pallas kernels, body(): call(start, 'start', [((EXT, *vecs), F32), ((2, NEAR, *vecs), F32), ((2,...  7.96 us
    ppermute x1, starting transfers between devices, body(): got_b = lax.ppermute(msg_b, AXES, route_b)  6.55 us
    pallas_call x1, Pallas kernels, body(): call(edges, 'edges', [(side, F32), (side, F32), packed, packed] + [((coun...  3.93 us
    pallas_call x1, Pallas kernels, body(): call(tail, 'tail', full, 8, [pltpu.VMEM((32, *vecs), F32)] * 2 + [pltpu.V...  3.88 us
    ppermute x1, starting transfers between devices, body(): rim_1 = lax.ppermute(rim, AXES, route_1)  3.39 us
    ppermute x1, waiting for transfers between devices, body(): got_b = lax.ppermute(msg_b, AXES, route_b)  2.37 us
    pallas_call x1, Pallas kernels, body(): call(near_rows, 'near_rows', [((32, *vecs), F32)], 3, limit=4)  0.99 us
    pallas_call x1, Pallas kernels, body(): ens, clim = call(main, 'main', most, 2, limit=5)(state, into_v)  0.95 us
  transfers between devices with their start and end apart: 6, of which 1 were waited for; matrix products, arithmetic and copies ran while one was open for 0% of the time, Pallas kernels for 30%

profile of v2, /device:TPU:29, one launch (start us, length us, event | category | flops | bytes accessed | tf_op | source)
XLA Modules:
  0.0 33.6 jit_solution(14117055257870422929)
XLA Ops:
  0.6 3.9 %edges.1 = (f32[6,9,8,128]{3,2,1,0:T(8,128)S(1)}, f32[6,9,8,128]{3,2,1,0:T(8,128)S(1)}, f32[32,8,128]{2,1,0:T(8,128)S(1)}, f32[32,8,128]{2,1,0:T(8,128)S(1)}, bf...) custom-call(bf16[64,64,128]{2,1,0:T(8,128)(2,1)} %bitcast.2, ...), custom_call_target="tpu_custom_call" | custom-call | tf_op jit(solution)/shard_map/edges/pallas_call | solution.py:530
  4.6 0.8 %collective-permute-start.2 = (f32[32,8,128]{2,1,0:T(8,128)S(1)}, f32[32,8,128]{2,1,0:T(8,128)S(1)}, u32[]{:S(2)}, u32[]{:S(2)}) collective-permute-start(f32[32,8,128]{2,1,0:T(8,128)S(1)} %get-tuple-element.28), channel_id=1, source_target_pairs={{0,8},{1,9},{2,10},{3,11},{4,12},{5,13},{6,14},{7,15},{8,0},{9,1},... | collective-permute-start | bytes 393224 | tf_op jit(solution)/shard_map/ppermute | solution.py:546
  5.3 0.9 %collective-permute-start.3 = (f32[32,8,128]{2,1,0:T(8,128)S(1)}, f32[32,8,128]{2,1,0:T(8,128)S(1)}, u32[]{:S(2)}, u32[]{:S(2)}) collective-permute-start(f32[32,8,128]{2,1,0:T(8,128)S(1)} %get-tuple-element.29), channel_id=1, source_target_pairs={{0,248},{1,249},{2,250},{3,251},{4,252},{5,253},{6,254},{7,255},{8... | collective-permute-start | bytes 393224 | tf_op jit(solution)/shard_map/ppermute | solution.py:545
  6.2 0.5 %collective-permute-start = (f32[6,9,8,128]{3,2,1,0:T(8,128)S(1)}, f32[6,9,8,128]{3,2,1,0:T(8,128)S(1)}, u32[]{:S(2)}, u32[]{:S(2)}) collective-permute-start(f32[6,9,8,128]{3,2,1,0:T(8,128)S(1)} %get-tuple-element.26), channel_id=1, source_target_pairs={{0,1},{1,0},{2,3},{3,2},{4,5},{5,4},{6,7},{7,6},{8,9},{9,8},{10,11... | collective-permute-start | bytes 663560 | tf_op jit(solution)/shard_map/ppermute | solution.py:544
  6.7 6.5 %collective-permute-start.1 = (f32[6,9,8,128]{3,2,1,0:T(8,128)S(1)}, f32[6,9,8,128]{3,2,1,0:T(8,128)S(1)}, u32[]{:S(2)}, u32[]{:S(2)}) collective-permute-start(f32[6,9,8,128]{3,2,1,0:T(8,128)S(1)} %get-tuple-element.27), channel_id=1, source_target_pairs={{1,2},{2,1},{3,4},{4,3},{5,6},{6,5},{7,255},{9,10},{10,9},{11,12},... | collective-permute-start | bytes 663560 | tf_op jit(solution)/shard_map/ppermute | solution.py:543
  13.3 0.0 collective-permute-done.2.got_1
  13.3 0.0 collective-permute-done.3.got_2
  13.3 8.0 %start.1 = (f32[76,12,8,128]{3,2,1,0:T(8,128)S(1)}, f32[2,7,12,8,128]{4,3,2,1,0:T(8,128)S(1)}, f32[2,5,2,12,8,128]{5,4,3,2,1,0:T(8,128)S(1)}, f32[2,10,12,8,128]{4,3,2,1,0:T(8,128)S(1)}) custom-call(f32[64,12,8,128]{3,2,1,0:T(8,128)S(1)} %spread.1.own, f32[32,8,128]{2,1,0:T(8,128)S(1)} %collective-permute-done.2.got_1, ...), custom_call_target="tpu_custom_call" | custom-call | flops 99999997952 | bytes 100000000 | tf_op jit(solution)/shard_map/start/pallas_call | solution.py:552
  21.3 0.0 collective-permute-done.msg_a
  21.3 2.4 %collective-permute-done.1.msg_b = f32[6,9,8,128]{3,2,1,0:T(8,128)S(1)} collective-permute-done((f32[6,9,8,128]{3,2,1,0:T(8,128)S(1)}, f32[6,9,8,128]{3,2,1,0:T(8,128)S(1)}, u32[]{:S(2)}, u32[]{:S(2)}) %collective-permute-start.1) | collective-permute-done | bytes 221216 | tf_op jit(solution)/shard_map/ppermute | solution.py:543
  23.7 0.2 rim.1
  23.8 0.5 %collective-permute-start.5 = (f32[2,6,8,128]{3,2,1,0:T(8,128)S(1)}, f32[2,6,8,128]{3,2,1,0:T(8,128)S(1)}, u32[]{:S(2)}, u32[]{:S(2)}) collective-permute-start(f32[2,6,8,128]{3,2,1,0:T(8,128)S(1)} %rim.1), channel_id=1, source_target_pairs={{0,248},{1,249},{2,250},{3,251},{4,252},{5,253},{6,254},{7,255},{8... | collective-permute-start | bytes 147464 | tf_op jit(solution)/shard_map/ppermute | solution.py:565
  24.3 3.4 %collective-permute-start.4 = (f32[2,6,8,128]{3,2,1,0:T(8,128)S(1)}, f32[2,6,8,128]{3,2,1,0:T(8,128)S(1)}, u32[]{:S(2)}, u32[]{:S(2)}) collective-permute-start(f32[2,6,8,128]{3,2,1,0:T(8,128)S(1)} %rim.1), channel_id=1, source_target_pairs={{0,8},{1,9},{2,10},{3,11},{4,12},{5,13},{6,14},{7,15},{8,0},{9,1},... | collective-permute-start | bytes 147464 | tf_op jit(solution)/shard_map/ppermute | solution.py:564
  27.7 1.0 %main.1 = (bf16[64,32,128]{2,1,0:T(8,128)(2,1)S(1)}, f32[2,32,128]{2,1,0:T(8,128)S(1)}) custom-call(f32[76,12,8,128]{3,2,1,0:T(8,128)S(1)} %get-tuple-element.45.state, bf16[384,512]{1,0:T(8,128)(2,1)S(1)} %get-tuple-element.32.table), custom_call_target="tpu_custom_call" | custom-call | tf_op jit(solution)/shard_map/main/pallas_call | solution.py:570
  28.7 1.0 %near_rows.1.rows_in = f32[32,12,8,128]{3,2,1,0:T(8,128)S(1)} custom-call(f32[2,7,12,8,128]{4,3,2,1,0:T(8,128)S(1)} %get-tuple-element.42.near, f32[6,9,8,128]{3,2,1,0:T(8,128)S(1)} %collective-permute-done.msg_a, f32[6,9,8,128]{3,2,1,0:T(8,128)S(1)} %collective-permute-done.1.msg_b), custom_call_target="tpu_custom_call" | custom-call | tf_op jit(solution)/shard_map/near_rows/pallas_call | solution.py:569
  29.7 0.0 collective-permute-done.5.rim_2
  29.7 0.0 collective-permute-done.4.rim_1
  29.7 3.9 %tail.1 = (bf16[64,64,128]{2,1,0:T(8,128)(2,1)}, f32[2,64,128]{2,1,0:T(8,128)}) custom-call(f32[32,12,8,128]{3,2,1,0:T(8,128)S(1)} %near_rows.1.rows_in, f32[2,5,2,12,8,128]{5,4,3,2,1,0:T(8,128)S(1)} %get-tuple-element.43.kept, f32[2,10,12,8,128]{4,3,2,1,0:T(8,128)S(1)} %get-tuple-element.44.fin, f32[2,6,8,128]{3,2,1,0:T(8,128)S(1)} %collective-permute-done.4.rim_1, ...), custom_call_target="tpu_custom_call" | custom-call | tf_op jit(solution)/shard_map/tail/pallas_call | solution.py:571
  (1 shorter events, 0.0 us)
Async XLA Ops:
  4.6 8.7 %collective-permute-start.2 = (f32[32,8,128]{2,1,0:T(8,128)S(1)}, f32[32,8,128]{2,1,0:T(8,128)S(1)}, u32[]{:S(2)}, u32[]{:S(2)}) collective-permute-start(f32[32,8,128]{2,1,0:T(8,128)S(1)} %get-tuple-element.28), channel_id=1, source_target_pairs={{0,8},{1,9},{2,10},{3,11},{4,12},{5,13},{6,14},{7,15},{8,0},{9,1},... | collective-permute-start | bytes 393224 | tf_op jit(solution)/shard_map/ppermute | solution.py:546
  5.3 8.0 %collective-permute-start.3 = (f32[32,8,128]{2,1,0:T(8,128)S(1)}, f32[32,8,128]{2,1,0:T(8,128)S(1)}, u32[]{:S(2)}, u32[]{:S(2)}) collective-permute-start(f32[32,8,128]{2,1,0:T(8,128)S(1)} %get-tuple-element.29), channel_id=1, source_target_pairs={{0,248},{1,249},{2,250},{3,251},{4,252},{5,253},{6,254},{7,255},{8... | collective-permute-start | bytes 393224 | tf_op jit(solution)/shard_map/ppermute | solution.py:545
  6.2 15.0 %collective-permute-start = (f32[6,9,8,128]{3,2,1,0:T(8,128)S(1)}, f32[6,9,8,128]{3,2,1,0:T(8,128)S(1)}, u32[]{:S(2)}, u32[]{:S(2)}) collective-permute-start(f32[6,9,8,128]{3,2,1,0:T(8,128)S(1)} %get-tuple-element.26), channel_id=1, source_target_pairs={{0,1},{1,0},{2,3},{3,2},{4,5},{5,4},{6,7},{7,6},{8,9},{9,8},{10,11... | collective-permute-start | bytes 663560 | tf_op jit(solution)/shard_map/ppermute | solution.py:544
  6.7 16.9 %collective-permute-start.1 = (f32[6,9,8,128]{3,2,1,0:T(8,128)S(1)}, f32[6,9,8,128]{3,2,1,0:T(8,128)S(1)}, u32[]{:S(2)}, u32[]{:S(2)}) collective-permute-start(f32[6,9,8,128]{3,2,1,0:T(8,128)S(1)} %get-tuple-element.27), channel_id=1, source_target_pairs={{1,2},{2,1},{3,4},{4,3},{5,6},{6,5},{7,255},{9,10},{10,9},{11,12},... | collective-permute-start | bytes 663560 | tf_op jit(solution)/shard_map/ppermute | solution.py:543
  23.8 5.8 %collective-permute-start.5 = (f32[2,6,8,128]{3,2,1,0:T(8,128)S(1)}, f32[2,6,8,128]{3,2,1,0:T(8,128)S(1)}, u32[]{:S(2)}, u32[]{:S(2)}) collective-permute-start(f32[2,6,8,128]{3,2,1,0:T(8,128)S(1)} %rim.1), channel_id=1, source_target_pairs={{0,248},{1,249},{2,250},{3,251},{4,252},{5,253},{6,254},{7,255},{8... | collective-permute-start | bytes 147464 | tf_op jit(solution)/shard_map/ppermute | solution.py:565
  24.3 5.4 %collective-permute-start.4 = (f32[2,6,8,128]{3,2,1,0:T(8,128)S(1)}, f32[2,6,8,128]{3,2,1,0:T(8,128)S(1)}, u32[]{:S(2)}, u32[]{:S(2)}) collective-permute-start(f32[2,6,8,128]{3,2,1,0:T(8,128)S(1)} %rim.1), channel_id=1, source_target_pairs={{0,8},{1,9},{2,10},{3,11},{4,12},{5,13},{6,14},{7,15},{8,0},{9,1},... | collective-permute-start | bytes 147464 | tf_op jit(solution)/shard_map/ppermute | solution.py:564

commit v3 on v2

--- a/solution.py
+++ b/solution.py
@@ -125,8 +125,11 @@
             for k in range(STEPS):
                 side_rows[side, k, g] = block[7 - k if side else k]
     a_side = jnp.where(odd, 0, 1)
-    msg_a[...] = side_rows[a_side]
-    msg_b[...] = side_rows[1 - a_side]
+    for msg, which in ((msg_a, a_side), (msg_b, 1 - a_side)):
+        msg[0 : 8 * STEPS] = side_rows[which, :, 0:8].reshape(8 * STEPS, *TILE)
+        for k in range(0, STEPS, 2):
+            two = side_rows[which, k, 8] + pltpu.roll(side_rows[which, k + 1, 8], 4, 0)
+            msg[8 * STEPS + k // 2] = two
 
     column = rim_column()
     ensemble = lax.rem(lane, HALF) < 8 * STEPS
@@ -163,6 +166,11 @@
         deal(mem_v, src_v, into_v, own)
 
 
+def row_groups(msg, k):
+    two = msg[8 * STEPS + k // 2]
+    return [msg[8 * k + g] for g in range(8)] + [pltpu.roll(two, 4, 0) if k % 2 else two]
+
+
 def rim_column():
     lane = lanes()
     n = lax.rem(lax.rem(lane, HALF), STEPS)
@@ -233,9 +241,10 @@
     for side, msg in enumerate((msg_a, msg_b)):
         index = jnp.where(fold, LANES - 1 - column, column) if side else column
         for k in range(STEPS):
-            acc = gather(msg[k, 0], index)
+            x = row_groups(msg, k)
+            acc = gather(x[0], index)
             for g in range(1, GROUPS):
-                acc = jnp.where(group == g, gather(msg[k, g], index), acc)
+                acc = jnp.where(group == g, gather(x[g], index), acc)
             rim[side, k] = acc
 
 
@@ -254,7 +263,7 @@
         for n in range(NEAR):
             rows[16 * side + n] = near[side, n]
         for k in range(STEPS):
-            x = [msg[k, g] for g in range(GROUPS)]
+            x = row_groups(msg, k)
             for t in range(SETS):
                 for p in range(PHASES):
                     column = places[side][p][0]
@@ -332,32 +341,36 @@
     return out
 
 
-def finish(row, odd, table, ens_out, clim_out, rows):
+def finish(tiles, table):
     lane = lanes()
     index = 2 * SPAN + (lane + STEPS) // PHASES
     phase = lax.rem(lane + STEPS, PHASES)
     for t in range(SETS):
-        blocks = []
-        for p in range(PHASES):
-            halves = []
-            for h in range(2):
-                x = jnp.stack([row(8 * h + e, PHASES * t + p) for e in range(8)])
-                halves.append(jnp.swapaxes(x, 0, 1))
-            blocks.append(jnp.concatenate(halves, axis=1))
-        if t == 2:
-            for v in range(2):
+        lhs = []
+        for row, _, clim_out, rows in tiles:
+            blocks = []
+            for p in range(PHASES):
                 halves = []
                 for h in range(2):
-                    cut = slice(8 * h, 8 * h + 8)
-                    x = gather(blocks[0][v, cut], index)
-                    for p in range(1, PHASES):
-                        x = jnp.where(phase == p, gather(blocks[p][v, cut], index), x)
-                    halves.append(x)
-                clim_out[v, rows, :] = jnp.concatenate(halves, axis=0)
-        lhs = jnp.concatenate([x.astype(BF16).reshape(8 * 16, LANES) for x in blocks], axis=1)
-        out = dot(lhs, table[...], 1).astype(BF16)
-        for k in range(3 if t < 2 else 2):
-            ens_out[pl.ds(8 * (3 * t + k), 8), rows, :] = out[:, LANES * k : LANES * k + LANES].reshape(8, 16, LANES)
+                    x = jnp.stack([row(8 * h + e, PHASES * t + p) for e in range(8)])
+                    halves.append(jnp.swapaxes(x, 0, 1))
+                blocks.append(jnp.concatenate(halves, axis=1))
+            if t == 2:
+                for v in range(2):
+                    halves = []
+                    for h in range(2):
+                        cut = slice(8 * h, 8 * h + 8)
+                        x = gather(blocks[0][v, cut], index)
+                        for p in range(1, PHASES):
+                            x = jnp.where(phase == p, gather(blocks[p][v, cut], index), x)
+                        halves.append(x)
+                    clim_out[v, rows, :] = jnp.concatenate(halves, axis=0)
+            lhs.append(jnp.concatenate([x.astype(BF16).reshape(8 * 16, LANES) for x in blocks], axis=1))
+        out = dot(jnp.concatenate(lhs, axis=0), table[...], 1).astype(BF16)
+        for n, (_, ens_out, _, rows) in enumerate(tiles):
+            for k in range(3 if t < 2 else 2):
+                x = out[LANES * n : LANES * n + LANES, LANES * k : LANES * k + LANES].reshape(8, 16, LANES)
+                ens_out[pl.ds(8 * (3 * t + k), 8), rows, :] = x
 
 
 FIN = 16 - STEPS
@@ -431,15 +444,11 @@
 def main(state, table, ens, clim):
     odd = is_odd()
 
-    def tile(m, _):
-        def row(n, q):
-            r = 16 * m + 16 + n
-            return state[STEPS + jnp.where(odd, r, ROWS - 1 - r), q]
-
-        finish(row, odd, table, ens, clim, row_tile(m))
-        return 0
-
-    lax.fori_loop(0, ROWS // 16 - 2, tile, 0)
+    def row(n, q, m):
+        r = 16 * m + 16 + n
+        return state[STEPS + jnp.where(odd, r, ROWS - 1 - r), q]
+
+    finish([(functools.partial(row, m=m), ens, clim, pl.ds(16 * m, 16)) for m in range(2)], table)
 
 
 def tail(
@@ -488,10 +497,10 @@
             two[16 * side + FIN + n] = one[16 * side + 1 + n]
         rising = odd if side else ~odd
 
-        def row(n, q):
+        def row(n, q, side=side, rising=rising):
             return two[16 * side + jnp.where(rising, n, 15 - n), q]
 
-        finish(row, odd, table, ens_rows.at[side], clim_rows.at[side], pl.ds(0, 16))
+        finish([(row, ens_rows.at[side], clim_rows.at[side], pl.ds(0, 16))], table)
         rows = row_tile(jnp.where(rising, ROWS // 16 - 1, 0))
         copies += [
             pltpu.make_async_copy(ens_rows.at[side], ens.at[:, rows, :], sem.at[2 + 2 * side]),
@@ -524,13 +533,14 @@
     count = members.shape[0] * 2
     arrays = (members.reshape(count, ROWS, LANES), increment, climate_spread, diffusivity, inverse_area, land_sea)
     side = (STEPS, GROUPS, *TILE)
+    message = (8 * STEPS + STEPS // 2, *TILE)
     hbm = [pl.BlockSpec(memory_space=pltpu.HBM)] * 9
     two = (2, ROWS, LANES)
     packed = ((ROWS // 2, *TILE), F32)
     msg_a, msg_b, msg_1, msg_2, mem_v, src_v, into_v, tab_h_v, own = call(
         edges,
         "edges",
-        [(side, F32), (side, F32), packed, packed]
+        [(message, F32), (message, F32), packed, packed]
         + [((count, ROWS, LANES), BF16), ((6, ROWS, LANES), F32), (table_in.shape, BF16), (table_halo.shape, BF16)]
         + [((ROWS, VECS, *TILE), F32)],
         9,

time: 33.9 us -> 33.6 us (level)
  the two profiles are of different devices: /device:TPU:29 before, /device:TPU:24 now
where the time goes in v3:
time: 33.6 us; the launch traced here: 33.5 us
  Pallas kernels  17.5 us (52%)
  starting transfers between devices  11.7 us (35%)
  waiting for transfers between devices  3.52 us (10%)
  between operations  0.71 us (2%)
    pallas_call x1, Pallas kernels, body(): call(start, 'start', [((EXT, *vecs), F32), ((2, NEAR, *vecs), F32), ((2,...  7.96 us
    ppermute x1, starting transfers between devices, body(): got_2 = lax.ppermute(msg_2, AXES, route_2)  5.13 us
    ppermute x1, starting transfers between devices, body(): got_b = lax.ppermute(msg_b, AXES, route_b)  5.11 us
    pallas_call x1, Pallas kernels, body(): call(edges, 'edges', [(message, F32), (message, F32), packed, packed] + [...  3.94 us
    pallas_call x1, Pallas kernels, body(): call(tail, 'tail', full, 8, [pltpu.VMEM((32, *vecs), F32)] * 2 + [pltpu.V...  3.88 us
    ppermute x1, waiting for transfers between devices, body(): rim_2 = lax.ppermute(rim, AXES, route_2)  3.5 us
    pallas_call x1, Pallas kernels, body(): call(near_rows, 'near_rows', [((32, *vecs), F32)], 3, limit=4)  0.99 us
    ppermute x1, starting transfers between devices, body(): got_a = lax.ppermute(msg_a, AXES, route_a)  0.75 us
  transfers between devices with their start and end apart: 6, of which 1 were waited for; matrix products, arithmetic and copies ran while one was open for 0% of the time, Pallas kernels for 28%

profile of v3, /device:TPU:24, one launch (start us, length us, event | category | flops | bytes accessed | tf_op | source)
XLA Modules:
  0.0 33.5 jit_solution(7130398295663558879)
XLA Ops:
  0.6 3.9 %edges.1 = (f32[51,8,128]{2,1,0:T(8,128)S(1)}, f32[51,8,128]{2,1,0:T(8,128)S(1)}, f32[32,8,128]{2,1,0:T(8,128)S(1)}, f32[32,8,128]{2,1,0:T(8,128)S(1)}, bf16[64,...) custom-call(bf16[64,64,128]{2,1,0:T(8,128)(2,1)} %bitcast.2, ...), custom_call_target="tpu_custom_call" | custom-call | tf_op jit(solution)/shard_map/edges/pallas_call | solution.py:540
  4.6 0.1 collective-permute-start.2
  4.7 5.1 %collective-permute-start.3 = (f32[32,8,128]{2,1,0:T(8,128)S(1)}, f32[32,8,128]{2,1,0:T(8,128)S(1)}, u32[]{:S(2)}, u32[]{:S(2)}) collective-permute-start(f32[32,8,128]{2,1,0:T(8,128)S(1)} %get-tuple-element.29), channel_id=1, source_target_pairs={{0,248},{1,249},{2,250},{3,251},{4,252},{5,253},{6,254},{7,255},{8... | collective-permute-start | bytes 393224 | tf_op jit(solution)/shard_map/ppermute | solution.py:555
  9.8 0.8 %collective-permute-start = (f32[51,8,128]{2,1,0:T(8,128)S(1)}, f32[51,8,128]{2,1,0:T(8,128)S(1)}, u32[]{:S(2)}, u32[]{:S(2)}) collective-permute-start(f32[51,8,128]{2,1,0:T(8,128)S(1)} %get-tuple-element.26), channel_id=1, source_target_pairs={{0,1},{1,0},{2,3},{3,2},{4,5},{5,4},{6,7},{7,6},{8,9},{9,8},{10,11... | collective-permute-start | bytes 626696 | tf_op jit(solution)/shard_map/ppermute | solution.py:554
  10.6 5.1 %collective-permute-start.1 = (f32[51,8,128]{2,1,0:T(8,128)S(1)}, f32[51,8,128]{2,1,0:T(8,128)S(1)}, u32[]{:S(2)}, u32[]{:S(2)}) collective-permute-start(f32[51,8,128]{2,1,0:T(8,128)S(1)} %get-tuple-element.27), channel_id=1, source_target_pairs={{1,2},{2,1},{3,4},{4,3},{5,6},{6,5},{7,255},{9,10},{10,9},{11,12},... | collective-permute-start | bytes 626696 | tf_op jit(solution)/shard_map/ppermute | solution.py:553
  15.7 0.0 collective-permute-done.2.got_1
  15.7 0.0 collective-permute-done.3.got_2
  15.7 8.0 %start.1 = (f32[76,12,8,128]{3,2,1,0:T(8,128)S(1)}, f32[2,7,12,8,128]{4,3,2,1,0:T(8,128)S(1)}, f32[2,5,2,12,8,128]{5,4,3,2,1,0:T(8,128)S(1)}, f32[2,10,12,8,128]{4,3,2,1,0:T(8,128)S(1)}) custom-call(f32[64,12,8,128]{3,2,1,0:T(8,128)S(1)} %spread.1.own, f32[32,8,128]{2,1,0:T(8,128)S(1)} %collective-permute-done.2.got_1, ...), custom_call_target="tpu_custom_call" | custom-call | flops 99999997952 | bytes 100000000 | tf_op jit(solution)/shard_map/start/pallas_call | solution.py:562
  23.7 0.0 collective-permute-done.msg_a
  23.7 0.0 collective-permute-done.1.msg_b
  23.7 0.2 rim.1
  23.9 0.7 %collective-permute-start.5 = (f32[2,6,8,128]{3,2,1,0:T(8,128)S(1)}, f32[2,6,8,128]{3,2,1,0:T(8,128)S(1)}, u32[]{:S(2)}, u32[]{:S(2)}) collective-permute-start(f32[2,6,8,128]{3,2,1,0:T(8,128)S(1)} %rim.1), channel_id=1, source_target_pairs={{0,248},{1,249},{2,250},{3,251},{4,252},{5,253},{6,254},{7,255},{8... | collective-permute-start | bytes 147464 | tf_op jit(solution)/shard_map/ppermute | solution.py:575
  24.6 0.0 collective-permute-start.4
  24.6 0.5 %main.1 = (bf16[64,32,128]{2,1,0:T(8,128)(2,1)S(1)}, f32[2,32,128]{2,1,0:T(8,128)S(1)}) custom-call(f32[76,12,8,128]{3,2,1,0:T(8,128)S(1)} %get-tuple-element.45.state, bf16[384,512]{1,0:T(8,128)(2,1)S(1)} %get-tuple-element.32.table), custom_call_target="tpu_custom_call" | custom-call | tf_op jit(solution)/shard_map/main/pallas_call | solution.py:580
  25.1 1.0 %near_rows.1.rows_in = f32[32,12,8,128]{3,2,1,0:T(8,128)S(1)} custom-call(f32[2,7,12,8,128]{4,3,2,1,0:T(8,128)S(1)} %get-tuple-element.42.near, f32[51,8,128]{2,1,0:T(8,128)S(1)} %collective-permute-done.msg_a, f32[51,8,128]{2,1,0:T(8,128)S(1)} %collective-permute-done.1.msg_b), custom_call_target="tpu_custom_call" | custom-call | tf_op jit(solution)/shard_map/near_rows/pallas_call | solution.py:579
  26.1 3.5 %collective-permute-done.5.rim_2 = f32[2,6,8,128]{3,2,1,0:T(8,128)S(1)} collective-permute-done((f32[2,6,8,128]{3,2,1,0:T(8,128)S(1)}, f32[2,6,8,128]{3,2,1,0:T(8,128)S(1)}, u32[]{:S(2)}, u32[]{:S(2)}) %collective-permute-start.5) | collective-permute-done | bytes 49184 | tf_op jit(solution)/shard_map/ppermute | solution.py:575
  29.6 0.0 collective-permute-done.4.rim_1
  29.6 3.9 %tail.1 = (bf16[64,64,128]{2,1,0:T(8,128)(2,1)}, f32[2,64,128]{2,1,0:T(8,128)}) custom-call(f32[32,12,8,128]{3,2,1,0:T(8,128)S(1)} %near_rows.1.rows_in, f32[2,5,2,12,8,128]{5,4,3,2,1,0:T(8,128)S(1)} %get-tuple-element.43.kept, f32[2,10,12,8,128]{4,3,2,1,0:T(8,128)S(1)} %get-tuple-element.44.fin, f32[2,6,8,128]{3,2,1,0:T(8,128)S(1)} %collective-permute-done.4.rim_1, ...), custom_call_target="tpu_custom_call" | custom-call | tf_op jit(solution)/shard_map/tail/pallas_call | solution.py:581
  (1 shorter events, 0.0 us)
Async XLA Ops:
  4.6 11.1 %collective-permute-start.2 = (f32[32,8,128]{2,1,0:T(8,128)S(1)}, f32[32,8,128]{2,1,0:T(8,128)S(1)}, u32[]{:S(2)}, u32[]{:S(2)}) collective-permute-start(f32[32,8,128]{2,1,0:T(8,128)S(1)} %get-tuple-element.28), channel_id=1, source_target_pairs={{0,8},{1,9},{2,10},{3,11},{4,12},{5,13},{6,14},{7,15},{8,0},{9,1},... | collective-permute-start | bytes 393224 | tf_op jit(solution)/shard_map/ppermute | solution.py:556
  4.7 11.0 %collective-permute-start.3 = (f32[32,8,128]{2,1,0:T(8,128)S(1)}, f32[32,8,128]{2,1,0:T(8,128)S(1)}, u32[]{:S(2)}, u32[]{:S(2)}) collective-permute-start(f32[32,8,128]{2,1,0:T(8,128)S(1)} %get-tuple-element.29), channel_id=1, source_target_pairs={{0,248},{1,249},{2,250},{3,251},{4,252},{5,253},{6,254},{7,255},{8... | collective-permute-start | bytes 393224 | tf_op jit(solution)/shard_map/ppermute | solution.py:555
  9.8 13.9 %collective-permute-start = (f32[51,8,128]{2,1,0:T(8,128)S(1)}, f32[51,8,128]{2,1,0:T(8,128)S(1)}, u32[]{:S(2)}, u32[]{:S(2)}) collective-permute-start(f32[51,8,128]{2,1,0:T(8,128)S(1)} %get-tuple-element.26), channel_id=1, source_target_pairs={{0,1},{1,0},{2,3},{3,2},{4,5},{5,4},{6,7},{7,6},{8,9},{9,8},{10,11... | collective-permute-start | bytes 626696 | tf_op jit(solution)/shard_map/ppermute | solution.py:554
  10.6 13.1 %collective-permute-start.1 = (f32[51,8,128]{2,1,0:T(8,128)S(1)}, f32[51,8,128]{2,1,0:T(8,128)S(1)}, u32[]{:S(2)}, u32[]{:S(2)}) collective-permute-start(f32[51,8,128]{2,1,0:T(8,128)S(1)} %get-tuple-element.27), channel_id=1, source_target_pairs={{1,2},{2,1},{3,4},{4,3},{5,6},{6,5},{7,255},{9,10},{10,9},{11,12},... | collective-permute-start | bytes 626696 | tf_op jit(solution)/shard_map/ppermute | solution.py:553
  23.9 5.7 %collective-permute-start.5 = (f32[2,6,8,128]{3,2,1,0:T(8,128)S(1)}, f32[2,6,8,128]{3,2,1,0:T(8,128)S(1)}, u32[]{:S(2)}, u32[]{:S(2)}) collective-permute-start(f32[2,6,8,128]{3,2,1,0:T(8,128)S(1)} %rim.1), channel_id=1, source_target_pairs={{0,248},{1,249},{2,250},{3,251},{4,252},{5,253},{6,254},{7,255},{8... | collective-permute-start | bytes 147464 | tf_op jit(solution)/shard_map/ppermute | solution.py:575
  24.6 5.1 %collective-permute-start.4 = (f32[2,6,8,128]{3,2,1,0:T(8,128)S(1)}, f32[2,6,8,128]{3,2,1,0:T(8,128)S(1)}, u32[]{:S(2)}, u32[]{:S(2)}) collective-permute-start(f32[2,6,8,128]{3,2,1,0:T(8,128)S(1)} %rim.1), channel_id=1, source_target_pairs={{0,8},{1,9},{2,10},{3,11},{4,12},{5,13},{6,14},{7,15},{8,0},{9,1},... | collective-permute-start | bytes 147464 | tf_op jit(solution)/shard_map/ppermute | solution.py:574

commit v4 on v3

--- a/solution.py
+++ b/solution.py
@@ -288,7 +288,7 @@
     return [x[p - 1] if p else pltpu.roll(x[PHASES - 1], 1, 1) for p in range(PHASES)]
 
 
-def weigh(state, count, lo, hi, ground, dense, coef, unroll):
+def weigh(state, count, lo, hi, ground, dense, coef, unroll, starts=(0,)):
     lane = lanes()
     index = 2 * SPAN + lane - SPAN * (lane // SPAN)
     rows = flat(state)
@@ -322,7 +322,8 @@
 
     def expand(r, _):
         for n in range(5 * PHASES):
-            coef[r, n] = jnp.broadcast_to(dense[n, pl.ds(r, 1), :], TILE)
+            for first in starts:
+                coef[first + r, n] = jnp.broadcast_to(dense[n, pl.ds(first + r, 1), :], TILE)
         return 0
 
     lax.fori_loop(lo, hi, expand, 0, unroll=unroll)
@@ -477,7 +478,7 @@
                     _, is_halo, place = places[p]
                     x = gather(cor, place + SETS * STEPS * t)
                     one[r, PHASES * t + p] = jnp.where(is_halo, x, rows_in[r, PHASES * t + p])
-    weigh(one, 32, 1, 31, ground, dense, coef, 10)
+    weigh(one, 32, 1, NEAR + STEPS - 1, ground, dense, coef, 11, (0, 16))
     for s in range(STEPS):
         src, dst = (one, two) if s % 2 == 0 else (two, one)
         lo = NEAR - 1 - s

time: 33.6 us -> 33.1 us (0.985)
  Pallas kernels: 17.5 us -> 17 us
    pallas_call x1, Pallas kernels: 3.88 us -> 3.38 us  [body(): call(tail, 'tail', full, 8, [pltpu.VMEM((32, *vecs), F32)] * 2 + [pltpu.V...]
  transfers between devices with their start and end apart: 6 -> 6, of which waited for: 1 -> 1; matrix products, arithmetic and copies ran while one was open for 0% -> 0% of each run, Pallas kernels for 28% -> 29%
where the time goes in v4:
time: 33.1 us; the launch traced here: 33 us
  Pallas kernels  17 us (51%)
  starting transfers between devices  11.7 us (35%)
  waiting for transfers between devices  3.52 us (11%)
  between operations  0.71 us (2%)
    pallas_call x1, Pallas kernels, body(): call(start, 'start', [((EXT, *vecs), F32), ((2, NEAR, *vecs), F32), ((2,...  7.96 us
    ppermute x1, starting transfers between devices, body(): got_2 = lax.ppermute(msg_2, AXES, route_2)  5.13 us
    ppermute x1, starting transfers between devices, body(): got_b = lax.ppermute(msg_b, AXES, route_b)  5.11 us
    pallas_call x1, Pallas kernels, body(): call(edges, 'edges', [(message, F32), (message, F32), packed, packed] + [...  3.94 us
    ppermute x1, waiting for transfers between devices, body(): rim_2 = lax.ppermute(rim, AXES, route_2)  3.5 us
    pallas_call x1, Pallas kernels, body(): call(tail, 'tail', full, 8, [pltpu.VMEM((32, *vecs), F32)] * 2 + [pltpu.V...  3.38 us
    pallas_call x1, Pallas kernels, body(): call(near_rows, 'near_rows', [((32, *vecs), F32)], 3, limit=4)  0.99 us
    ppermute x1, starting transfers between devices, body(): got_a = lax.ppermute(msg_a, AXES, route_a)  0.75 us
  transfers between devices with their start and end apart: 6, of which 1 were waited for; matrix products, arithmetic and copies ran while one was open for 0% of the time, Pallas kernels for 29%

profile of v4, /device:TPU:24, one launch (start us, length us, event | category | flops | bytes accessed | tf_op | source)
XLA Modules:
  0.0 33.0 jit_solution(17079484256674348120)
XLA Ops:
  0.6 3.9 %edges.1 = (f32[51,8,128]{2,1,0:T(8,128)S(1)}, f32[51,8,128]{2,1,0:T(8,128)S(1)}, f32[32,8,128]{2,1,0:T(8,128)S(1)}, f32[32,8,128]{2,1,0:T(8,128)S(1)}, bf16[64,...) custom-call(bf16[64,64,128]{2,1,0:T(8,128)(2,1)} %bitcast.2, ...), custom_call_target="tpu_custom_call" | custom-call | tf_op jit(solution)/shard_map/edges/pallas_call | solution.py:541
  4.6 0.1 collective-permute-start.2
  4.7 5.1 %collective-permute-start.3 = (f32[32,8,128]{2,1,0:T(8,128)S(1)}, f32[32,8,128]{2,1,0:T(8,128)S(1)}, u32[]{:S(2)}, u32[]{:S(2)}) collective-permute-start(f32[32,8,128]{2,1,0:T(8,128)S(1)} %get-tuple-element.29), channel_id=1, source_target_pairs={{0,248},{1,249},{2,250},{3,251},{4,252},{5,253},{6,254},{7,255},{8... | collective-permute-start | bytes 393224 | tf_op jit(solution)/shard_map/ppermute | solution.py:556
  9.8 0.8 %collective-permute-start = (f32[51,8,128]{2,1,0:T(8,128)S(1)}, f32[51,8,128]{2,1,0:T(8,128)S(1)}, u32[]{:S(2)}, u32[]{:S(2)}) collective-permute-start(f32[51,8,128]{2,1,0:T(8,128)S(1)} %get-tuple-element.26), channel_id=1, source_target_pairs={{0,1},{1,0},{2,3},{3,2},{4,5},{5,4},{6,7},{7,6},{8,9},{9,8},{10,11... | collective-permute-start | bytes 626696 | tf_op jit(solution)/shard_map/ppermute | solution.py:555
  10.6 5.1 %collective-permute-start.1 = (f32[51,8,128]{2,1,0:T(8,128)S(1)}, f32[51,8,128]{2,1,0:T(8,128)S(1)}, u32[]{:S(2)}, u32[]{:S(2)}) collective-permute-start(f32[51,8,128]{2,1,0:T(8,128)S(1)} %get-tuple-element.27), channel_id=1, source_target_pairs={{1,2},{2,1},{3,4},{4,3},{5,6},{6,5},{7,255},{9,10},{10,9},{11,12},... | collective-permute-start | bytes 626696 | tf_op jit(solution)/shard_map/ppermute | solution.py:554
  15.7 0.0 collective-permute-done.2.got_1
  15.7 0.0 collective-permute-done.3.got_2
  15.7 8.0 %start.1 = (f32[76,12,8,128]{3,2,1,0:T(8,128)S(1)}, f32[2,7,12,8,128]{4,3,2,1,0:T(8,128)S(1)}, f32[2,5,2,12,8,128]{5,4,3,2,1,0:T(8,128)S(1)}, f32[2,10,12,8,128]{4,3,2,1,0:T(8,128)S(1)}) custom-call(f32[64,12,8,128]{3,2,1,0:T(8,128)S(1)} %spread.1.own, f32[32,8,128]{2,1,0:T(8,128)S(1)} %collective-permute-done.2.got_1, ...), custom_call_target="tpu_custom_call" | custom-call | flops 99999997952 | bytes 100000000 | tf_op jit(solution)/shard_map/start/pallas_call | solution.py:563
  23.7 0.0 collective-permute-done.msg_a
  23.7 0.0 collective-permute-done.1.msg_b
  23.7 0.2 rim.1
  23.9 0.7 %collective-permute-start.5 = (f32[2,6,8,128]{3,2,1,0:T(8,128)S(1)}, f32[2,6,8,128]{3,2,1,0:T(8,128)S(1)}, u32[]{:S(2)}, u32[]{:S(2)}) collective-permute-start(f32[2,6,8,128]{3,2,1,0:T(8,128)S(1)} %rim.1), channel_id=1, source_target_pairs={{0,248},{1,249},{2,250},{3,251},{4,252},{5,253},{6,254},{7,255},{8... | collective-permute-start | bytes 147464 | tf_op jit(solution)/shard_map/ppermute | solution.py:576
  24.6 0.0 collective-permute-start.4
  24.6 0.5 %main.1 = (bf16[64,32,128]{2,1,0:T(8,128)(2,1)S(1)}, f32[2,32,128]{2,1,0:T(8,128)S(1)}) custom-call(f32[76,12,8,128]{3,2,1,0:T(8,128)S(1)} %get-tuple-element.45.state, bf16[384,512]{1,0:T(8,128)(2,1)S(1)} %get-tuple-element.32.table), custom_call_target="tpu_custom_call" | custom-call | tf_op jit(solution)/shard_map/main/pallas_call | solution.py:581
  25.1 1.0 %near_rows.1.rows_in = f32[32,12,8,128]{3,2,1,0:T(8,128)S(1)} custom-call(f32[2,7,12,8,128]{4,3,2,1,0:T(8,128)S(1)} %get-tuple-element.42.near, f32[51,8,128]{2,1,0:T(8,128)S(1)} %collective-permute-done.msg_a, f32[51,8,128]{2,1,0:T(8,128)S(1)} %collective-permute-done.1.msg_b), custom_call_target="tpu_custom_call" | custom-call | tf_op jit(solution)/shard_map/near_rows/pallas_call | solution.py:580
  26.1 3.5 %collective-permute-done.5.rim_2 = f32[2,6,8,128]{3,2,1,0:T(8,128)S(1)} collective-permute-done((f32[2,6,8,128]{3,2,1,0:T(8,128)S(1)}, f32[2,6,8,128]{3,2,1,0:T(8,128)S(1)}, u32[]{:S(2)}, u32[]{:S(2)}) %collective-permute-start.5) | collective-permute-done | bytes 49184 | tf_op jit(solution)/shard_map/ppermute | solution.py:576
  29.6 0.0 collective-permute-done.4.rim_1
  29.6 3.4 %tail.1 = (bf16[64,64,128]{2,1,0:T(8,128)(2,1)}, f32[2,64,128]{2,1,0:T(8,128)}) custom-call(f32[32,12,8,128]{3,2,1,0:T(8,128)S(1)} %near_rows.1.rows_in, f32[2,5,2,12,8,128]{5,4,3,2,1,0:T(8,128)S(1)} %get-tuple-element.43.kept, f32[2,10,12,8,128]{4,3,2,1,0:T(8,128)S(1)} %get-tuple-element.44.fin, f32[2,6,8,128]{3,2,1,0:T(8,128)S(1)} %collective-permute-done.4.rim_1, ...), custom_call_target="tpu_custom_call" | custom-call | tf_op jit(solution)/shard_map/tail/pallas_call | solution.py:582
  (1 shorter events, 0.0 us)
Async XLA Ops:
  4.6 11.1 %collective-permute-start.2 = (f32[32,8,128]{2,1,0:T(8,128)S(1)}, f32[32,8,128]{2,1,0:T(8,128)S(1)}, u32[]{:S(2)}, u32[]{:S(2)}) collective-permute-start(f32[32,8,128]{2,1,0:T(8,128)S(1)} %get-tuple-element.28), channel_id=1, source_target_pairs={{0,8},{1,9},{2,10},{3,11},{4,12},{5,13},{6,14},{7,15},{8,0},{9,1},... | collective-permute-start | bytes 393224 | tf_op jit(solution)/shard_map/ppermute | solution.py:557
  4.7 11.0 %collective-permute-start.3 = (f32[32,8,128]{2,1,0:T(8,128)S(1)}, f32[32,8,128]{2,1,0:T(8,128)S(1)}, u32[]{:S(2)}, u32[]{:S(2)}) collective-permute-start(f32[32,8,128]{2,1,0:T(8,128)S(1)} %get-tuple-element.29), channel_id=1, source_target_pairs={{0,248},{1,249},{2,250},{3,251},{4,252},{5,253},{6,254},{7,255},{8... | collective-permute-start | bytes 393224 | tf_op jit(solution)/shard_map/ppermute | solution.py:556
  9.8 13.9 %collective-permute-start = (f32[51,8,128]{2,1,0:T(8,128)S(1)}, f32[51,8,128]{2,1,0:T(8,128)S(1)}, u32[]{:S(2)}, u32[]{:S(2)}) collective-permute-start(f32[51,8,128]{2,1,0:T(8,128)S(1)} %get-tuple-element.26), channel_id=1, source_target_pairs={{0,1},{1,0},{2,3},{3,2},{4,5},{5,4},{6,7},{7,6},{8,9},{9,8},{10,11... | collective-permute-start | bytes 626696 | tf_op jit(solution)/shard_map/ppermute | solution.py:555
  10.6 13.1 %collective-permute-start.1 = (f32[51,8,128]{2,1,0:T(8,128)S(1)}, f32[51,8,128]{2,1,0:T(8,128)S(1)}, u32[]{:S(2)}, u32[]{:S(2)}) collective-permute-start(f32[51,8,128]{2,1,0:T(8,128)S(1)} %get-tuple-element.27), channel_id=1, source_target_pairs={{1,2},{2,1},{3,4},{4,3},{5,6},{6,5},{7,255},{9,10},{10,9},{11,12},... | collective-permute-start | bytes 626696 | tf_op jit(solution)/shard_map/ppermute | solution.py:554
  23.9 5.7 %collective-permute-start.5 = (f32[2,6,8,128]{3,2,1,0:T(8,128)S(1)}, f32[2,6,8,128]{3,2,1,0:T(8,128)S(1)}, u32[]{:S(2)}, u32[]{:S(2)}) collective-permute-start(f32[2,6,8,128]{3,2,1,0:T(8,128)S(1)} %rim.1), channel_id=1, source_target_pairs={{0,248},{1,249},{2,250},{3,251},{4,252},{5,253},{6,254},{7,255},{8... | collective-permute-start | bytes 147464 | tf_op jit(solution)/shard_map/ppermute | solution.py:576
  24.6 5.1 %collective-permute-start.4 = (f32[2,6,8,128]{3,2,1,0:T(8,128)S(1)}, f32[2,6,8,128]{3,2,1,0:T(8,128)S(1)}, u32[]{:S(2)}, u32[]{:S(2)}) collective-permute-start(f32[2,6,8,128]{3,2,1,0:T(8,128)S(1)} %rim.1), channel_id=1, source_target_pairs={{0,8},{1,9},{2,10},{3,11},{4,12},{5,13},{6,14},{7,15},{8,0},{9,1},... | collective-permute-start | bytes 147464 | tf_op jit(solution)/shard_map/ppermute | solution.py:575
